TPU v7x, 32 devices: a whole 2x2x4 slice. The times are simulated.
32 devices in a mesh: rows: 8 (over z, y), seq: 4 (over x, core).
Axes of the slice: x: 2, y: 2, z: 4, core: 2. Of those that a mesh axis runs over, the one named last changes fastest.
Arguments:
- target: bfloat16 [16, 1024, 512], P('rows', 'seq'), may hold values from -6 to 6
- memory: bfloat16 [16, 1024, 512], P('rows', 'seq'), may hold values from -6 to 6
- tgt_group: int32 [16, 1024], P('rows', 'seq'), may hold values from -1 to 3, as said below
- src_group: int32 [16, 1024], P('rows', 'seq'), may hold values from -1 to 3, as said below
- self_qkv: bfloat16 [512, 1536], replicated, may hold values from -0.25 to 0.25
- self_out: bfloat16 [512, 512], replicated, may hold values from -1.5 to 1.5
- self_bias: float32 [3, 512], replicated, may hold values from -3 to 3
- cross_q: bfloat16 [512, 512], replicated, may hold values from -0.25 to 0.25
- cross_kv: bfloat16 [512, 1024], replicated, may hold values from -0.25 to 0.25
- cross_out: bfloat16 [512, 512], replicated, may hold values from -1.5 to 1.5
- cross_bias: float32 [3, 512], replicated, may hold values from -3 to 3
- ffn_in: bfloat16 [512, 2048], replicated, may hold values from -0.25 to 0.25
- ffn_in_bias: float32 [2048], replicated, may hold values from -3 to 3
- ffn_out: bfloat16 [2048, 512], replicated, may hold values from -0.125 to 0.125
- ffn_out_bias: float32 [512], replicated, may hold values from -3 to 3
- norm_gain: float32 [3, 512], replicated, may hold values from 0.5 to 1.5
- norm_bias: float32 [3, 512], replicated, may hold values from -3 to 3
- cotangent: bfloat16 [16, 1024, 512], P('rows', 'seq'), may hold values from -6 to 6
Outputs:
- layer_out: float32 [16, 1024, 512], P('rows', 'seq')
- d_target: float32 [16, 1024, 512], P('rows', 'seq')
- d_memory: float32 [16, 1024, 512], P('rows', 'seq')
- d_self_qkv: float32 [512, 1536], replicated
- d_self_out: float32 [512, 512], replicated
- d_self_bias: float32 [3, 512], replicated
- d_cross_q: float32 [512, 512], replicated
- d_cross_kv: float32 [512, 1024], replicated
- d_cross_out: float32 [512, 512], replicated
- d_cross_bias: float32 [3, 512], replicated
- d_ffn_in: float32 [512, 2048], replicated
- d_ffn_in_bias: float32 [2048], replicated
- d_ffn_out: float32 [2048, 512], replicated
- d_ffn_out_bias: float32 [512], replicated
- d_norm_gain: float32 [3, 512], replicated
- d_norm_bias: float32 [3, 512], replicated
Inputs may be any that keep to these rules, and one draw needn't show every extreme that they name: In every row, the positions hold documents 0 to 3 in order, then padding marked -1 (at least one position). One document of each row, which one drawn from the seed and the same number in tgt_group and src_group, begins within the first 256 positions and ends within the last 256. `src_group`: same law as tgt_group, with its own lengths; every document number of a row appears in both.
All inputs are finite; a program needn't handle non-finite values.
Results may differ from a plain program's by a relative error of at most 0.03.
Values may be sent and summed in bfloat16 or wider, within the bound.
No kernel may reach another device: no remote copies, remote signals or barrier semaphores. Data moves between devices by JAX's collectives and lax.ppermute only.
A program may use at most 256 MiB of HBM per device.

v0:
```python
import math

import jax
import jax.numpy as jnp
from jax import lax
from jax.sharding import PartitionSpec as P

HEADS = 8


eps_norm = 1e-05
score_scale = 0.125
lowest = -1e30


def layer_norm(hidden, scales, shifts):
    average = jnp.mean(hidden, axis=-1, keepdims=True)
    centred = hidden - average
    variance = jnp.mean(centred * centred, axis=-1, keepdims=True)
    return centred * lax.rsqrt(variance + eps_norm) * scales + shifts


def project(inputs, matrix):
    return jnp.einsum("rtd,de->rte", inputs, matrix, preferred_element_type=jnp.float32)


def weight_grad(inputs, grads):
    return jnp.einsum("rtd,rte->de", inputs, grads, preferred_element_type=jnp.float32)


def back_project(grads, matrix):
    return jnp.einsum("rte,de->rtd", grads, matrix, preferred_element_type=jnp.float32)


def column_sum(grads):
    return jnp.sum(grads.astype(jnp.float32), axis=(0, 1))


def allowed_mask(query_group, key_group, query_places, key_places, causal):
    allowed = query_group[:, None, :, None] == key_group[:, None, None, :]
    if causal:
        allowed = allowed & (key_places[None, None, None, :] <= query_places[None, None, :, None])
    return allowed


def block_loop(portion, states, needed, compute):
    length_here = portion[0].shape[1]
    block_size = math.gcd(length_here, 512)

    def one_block(states, number):
        begin_at = number * block_size
        blocks = tuple(
            (lax.dynamic_slice_in_dim(member, begin_at, block_size, 1) for member in portion)
        )
        if needed is None:
            states = compute(states, blocks, begin_at, block_size)
        else:
            states = lax.cond(
                needed(begin_at, block_size),
                lambda kept: compute(kept, blocks, begin_at, block_size),
                lambda kept: kept,
                states,
            )
        return (states, None)

    states, unused = lax.scan(one_block, states, jnp.arange(length_here // block_size))
    return states


def forward_step(queries, query_group, query_first, causal):
    query_places = query_first + jnp.arange(queries.shape[1])

    def compute(states, blocks, place, block_size):
        row_top, totals, accum_out = states
        key_block, value_block, group_block = blocks
        key_places = place + jnp.arange(block_size)
        scores = (
            jnp.einsum("rqhd,rkhd->rhqk", queries, key_block, preferred_element_type=jnp.float32)
            * score_scale
        )
        allowed = allowed_mask(query_group, group_block, query_places, key_places, causal)
        new_top = jnp.maximum(row_top, jnp.max(jnp.where(allowed, scores, lowest), axis=-1))
        factor = jnp.exp(row_top - new_top)
        weights = jnp.where(allowed, jnp.exp(scores - new_top[..., None]), 0.0)
        totals = totals * factor + jnp.sum(weights, axis=-1)
        update = jnp.einsum(
            "rhqk,rkhd->rqhd",
            weights.astype(jnp.bfloat16),
            value_block,
            preferred_element_type=jnp.float32,
        )
        accum_out = accum_out * jnp.swapaxes(factor, 1, 2)[..., None] + update
        return (new_top, totals, accum_out)

    def forward_before_last(place, block_size):
        return place <= query_places[-1]

    def forward_fold_keys(states, portion, offset):
        return block_loop(portion, states, forward_before_last if causal else None, compute)

    return forward_fold_keys


def backward_step(queries, grad_mixed, query_group, log_totals, deltas, query_first, causal):
    query_places = query_first + jnp.arange(queries.shape[1])

    def compute(states, blocks, place, block_size):
        key_block, value_block, group_block = blocks
        key_places = place + jnp.arange(block_size)
        scores = (
            jnp.einsum("rqhd,rkhd->rhqk", queries, key_block, preferred_element_type=jnp.float32)
            * score_scale
        )
        allowed = allowed_mask(query_group, group_block, query_places, key_places, causal)
        shares = jnp.where(allowed, jnp.exp(scores - log_totals[..., None]), 0.0)
        grad_shares = jnp.einsum(
            "rqhd,rkhd->rhqk", grad_mixed, value_block, preferred_element_type=jnp.float32
        )
        grad_scores = (shares * (grad_shares - deltas[..., None])).astype(jnp.bfloat16)
        grad_query = (
            states[0]
            + jnp.einsum(
                "rhqk,rkhd->rqhd", grad_scores, key_block, preferred_element_type=jnp.float32
            )
            * score_scale
        )
        grad_keys, grad_values = (states[1], states[2])
        key_part = (
            jnp.einsum("rhqk,rqhd->rkhd", grad_scores, queries, preferred_element_type=jnp.float32)
            * score_scale
        )
        value_part = jnp.einsum(
            "rhqk,rqhd->rkhd",
            shares.astype(jnp.bfloat16),
            grad_mixed,
            preferred_element_type=jnp.float32,
        )
        grad_keys = lax.dynamic_update_slice_in_dim(
            grad_keys,
            lax.dynamic_slice_in_dim(grad_keys, place, block_size, 1) + key_part,
            place,
            1,
        )
        grad_values = lax.dynamic_update_slice_in_dim(
            grad_values,
            lax.dynamic_slice_in_dim(grad_values, place, block_size, 1) + value_part,
            place,
            1,
        )
        return (grad_query, grad_keys, grad_values)

    def backward_before_last(place, block_size):
        return place <= query_places[-1]

    def backward_fold_keys(states, portion, offset):
        return block_loop(portion, states, backward_before_last if causal else None, compute)

    return backward_fold_keys


def finish(states):
    row_top, totals, accum_out = states
    mixed = accum_out / jnp.swapaxes(totals, 1, 2)[..., None]
    return (mixed, row_top + jnp.log(totals))


def per_device(
    target,
    memory,
    tgt_group,
    src_group,
    self_qkv,
    self_out,
    self_bias,
    cross_q,
    cross_kv,
    cross_out,
    cross_bias,
    ffn_in,
    ffn_in_bias,
    ffn_out,
    ffn_out_bias,
    norm_gain,
    norm_bias,
    cotangent,
):
    rows_here, length_here, model_width = target.shape
    head_size = model_width // HEADS
    row_length = length_here * lax.axis_size("seq")
    query_first = lax.axis_index("seq") * length_here

    def split_four(tensor):
        return tensor.reshape(rows_here, length_here, HEADS, head_size)

    def join_heads(tensor):
        return tensor.reshape(rows_here, length_here, model_width)

    def fresh_state():
        return (
            jnp.full((rows_here, HEADS, length_here), lowest, jnp.float32),
            jnp.zeros((rows_here, HEADS, length_here), jnp.float32),
            jnp.zeros((rows_here, length_here, HEADS, head_size), jnp.float32),
        )

    def own_zeros():
        return jnp.zeros((rows_here, length_here, HEADS, head_size), jnp.float32)

    def fresh_grads():
        return (
            own_zeros(),
            jnp.zeros((rows_here, row_length, HEADS, head_size), jnp.float32),
            jnp.zeros((rows_here, row_length, HEADS, head_size), jnp.float32),
        )

    def deltas_of(grad_mixed, mixed_full):
        return jnp.swapaxes(jnp.sum(grad_mixed.astype(jnp.float32) * mixed_full, axis=-1), 1, 2)

    tokens_full = target.astype(jnp.float32)
    projected = project(target, self_qkv)
    queries = split_four((projected[..., :model_width] + self_bias[0]).astype(jnp.bfloat16))
    key_rows = split_four(projected[..., model_width : 2 * model_width].astype(jnp.bfloat16))
    value_rows = split_four((projected[..., 2 * model_width :] + self_bias[1]).astype(jnp.bfloat16))
    self_forward = forward_step(queries, tgt_group, query_first, True)
    self_state = self_forward(
        fresh_state(),
        (
            lax.all_gather(key_rows, "seq", axis=1, tiled=True),
            lax.all_gather(value_rows, "seq", axis=1, tiled=True),
            lax.all_gather(tgt_group, "seq", axis=1, tiled=True),
        ),
        jnp.int32(0),
    )
    self_full, self_logs = finish(self_state)
    self_mixed = join_heads(self_full.astype(jnp.bfloat16))
    branch = project(self_mixed, self_out) + self_bias[2]
    first_norm, norm_one = jax.vjp(layer_norm, tokens_full + branch, norm_gain[0], norm_bias[0])
    first_low = first_norm.astype(jnp.bfloat16)
    cross_queries = split_four((project(first_low, cross_q) + cross_bias[0]).astype(jnp.bfloat16))
    cross_proj = project(memory, cross_kv)
    cross_keys = split_four(cross_proj[..., :model_width].astype(jnp.bfloat16))
    cross_values = split_four((cross_proj[..., model_width:] + cross_bias[1]).astype(jnp.bfloat16))
    cross_forward = forward_step(cross_queries, tgt_group, query_first, False)
    cross_state = cross_forward(
        fresh_state(),
        (
            lax.all_gather(cross_keys, "seq", axis=1, tiled=True),
            lax.all_gather(cross_values, "seq", axis=1, tiled=True),
            lax.all_gather(src_group, "seq", axis=1, tiled=True),
        ),
        jnp.int32(0),
    )
    cross_full, cross_logs = finish(cross_state)
    cross_mixed = join_heads(cross_full.astype(jnp.bfloat16))
    cross_branch = project(cross_mixed, cross_out) + cross_bias[2]
    second, norm_two = jax.vjp(layer_norm, first_norm + cross_branch, norm_gain[1], norm_bias[1])
    second_low = second.astype(jnp.bfloat16)
    pre_act = project(second_low, ffn_in) + ffn_in_bias
    inner_act, gelu_back = jax.vjp(jax.nn.gelu, pre_act)
    inner_low = inner_act.astype(jnp.bfloat16)
    outer_out = project(inner_low, ffn_out) + ffn_out_bias
    layer_out, norm_three = jax.vjp(layer_norm, second + outer_out, norm_gain[2], norm_bias[2])
    grad_three, gain_three, shift_three = norm_three(cotangent.astype(jnp.float32))
    grad_outer = grad_three.astype(jnp.bfloat16)
    d_ffn_out_bias = column_sum(grad_outer)
    d_ffn_out = weight_grad(inner_low, grad_outer)
    (grad_inner_pre,) = gelu_back(back_project(grad_outer, ffn_out))
    grad_pre = grad_inner_pre.astype(jnp.bfloat16)
    d_ffn_in_bias = column_sum(grad_pre)
    d_ffn_in = weight_grad(second_low, grad_pre)
    grad_second = grad_three + back_project(grad_pre, ffn_in)
    grad_two, gain_two, shift_two = norm_two(grad_second)
    grad_cross_branch = grad_two.astype(jnp.bfloat16)
    d_cross_out = weight_grad(cross_mixed, grad_cross_branch)
    grad_cross_mixed = split_four(back_project(grad_cross_branch, cross_out).astype(jnp.bfloat16))
    cross_deltas = deltas_of(grad_cross_mixed, cross_full)
    cross_backward = backward_step(
        cross_queries, grad_cross_mixed, tgt_group, cross_logs, cross_deltas, query_first, False
    )
    cross_grads = cross_backward(
        fresh_grads(),
        (
            lax.all_gather(cross_keys, "seq", axis=1, tiled=True),
            lax.all_gather(cross_values, "seq", axis=1, tiled=True),
            lax.all_gather(src_group, "seq", axis=1, tiled=True),
        ),
        jnp.int32(0),
    )
    cross_grad_query = cross_grads[0]
    cross_grad_keys, cross_grad_values = (
        lax.psum_scatter(
            cross_grads[1].astype(jnp.bfloat16), "seq", scatter_dimension=1, tiled=True
        ).astype(jnp.float32),
        lax.psum_scatter(
            cross_grads[2].astype(jnp.bfloat16), "seq", scatter_dimension=1, tiled=True
        ).astype(jnp.float32),
    )
    cross_dq = join_heads(cross_grad_query).astype(jnp.bfloat16)
    cross_dkv = jnp.concatenate(
        [
            join_heads(cross_grad_keys).astype(jnp.bfloat16),
            join_heads(cross_grad_values).astype(jnp.bfloat16),
        ],
        axis=-1,
    )
    d_cross_q = weight_grad(first_low, cross_dq)
    d_cross_kv = weight_grad(memory, cross_dkv)
    d_cross_bias = jnp.stack(
        [
            column_sum(cross_dq),
            column_sum(cross_dkv[..., model_width:]),
            column_sum(grad_cross_branch),
        ]
    )
    d_memory = back_project(cross_dkv, cross_kv)
    grad_first = grad_two + back_project(cross_dq, cross_q)
    grad_one, gain_one, shift_one = norm_one(grad_first)
    grad_self_branch = grad_one.astype(jnp.bfloat16)
    d_self_out = weight_grad(self_mixed, grad_self_branch)
    grad_self_mixed = split_four(back_project(grad_self_branch, self_out).astype(jnp.bfloat16))
    self_deltas = deltas_of(grad_self_mixed, self_full)
    self_backward = backward_step(
        queries, grad_self_mixed, tgt_group, self_logs, self_deltas, query_first, True
    )
    self_grads = self_backward(
        fresh_grads(),
        (
            lax.all_gather(key_rows, "seq", axis=1, tiled=True),
            lax.all_gather(value_rows, "seq", axis=1, tiled=True),
            lax.all_gather(tgt_group, "seq", axis=1, tiled=True),
        ),
        jnp.int32(0),
    )
    self_grad_query = self_grads[0]
    self_grad_keys, self_grad_values = (
        lax.psum_scatter(
            self_grads[1].astype(jnp.bfloat16), "seq", scatter_dimension=1, tiled=True
        ).astype(jnp.float32),
        lax.psum_scatter(
            self_grads[2].astype(jnp.bfloat16), "seq", scatter_dimension=1, tiled=True
        ).astype(jnp.float32),
    )
    self_dqkv = jnp.concatenate(
        [
            join_heads(self_grad_query).astype(jnp.bfloat16),
            join_heads(self_grad_keys).astype(jnp.bfloat16),
            join_heads(self_grad_values).astype(jnp.bfloat16),
        ],
        axis=-1,
    )
    d_self_qkv = weight_grad(target, self_dqkv)
    d_self_bias = jnp.stack(
        [
            column_sum(self_dqkv[..., :model_width]),
            column_sum(self_dqkv[..., 2 * model_width :]),
            column_sum(grad_self_branch),
        ]
    )
    d_target = grad_one + back_project(self_dqkv, self_qkv)
    d_norm_gain = jnp.stack([gain_one, gain_two, gain_three])
    d_norm_bias = jnp.stack([shift_one, shift_two, shift_three])
    summed = lax.psum(
        (
            d_self_qkv,
            d_self_out,
            d_self_bias,
            d_cross_q,
            d_cross_kv,
            d_cross_out,
            d_cross_bias,
            d_ffn_in,
            d_ffn_in_bias,
            d_ffn_out,
            d_ffn_out_bias,
            d_norm_gain,
            d_norm_bias,
        ),
        ("rows", "seq"),
    )
    return (layer_out, d_target, d_memory) + tuple(summed)


def solution(mesh):
    in_specs = (
        P("rows", "seq", None),
        P("rows", "seq", None),
        P("rows", "seq"),
        P("rows", "seq"),
        P(),
        P(),
        P(),
        P(),
        P(),
        P(),
        P(),
        P(),
        P(),
        P(),
        P(),
        P(),
        P(),
        P("rows", "seq", None),
    )
    out_specs = (
        P("rows", "seq", None),
        P("rows", "seq", None),
        P("rows", "seq", None),
        P(),
        P(),
        P(),
        P(),
        P(),
        P(),
        P(),
        P(),
        P(),
        P(),
        P(),
        P(),
        P(),
    )
    return jax.shard_map(
        per_device, mesh=mesh, in_specs=in_specs, out_specs=out_specs, check_vma=False
    )
```

profile of v0, /device:TPU:0, one launch (start us, length us, event | category | flops | bytes accessed | tf_op | source)
XLA Modules:
  0.0 771.9 jit_solution(10959888480968890599)
XLA Ops:
  23.1 6.1 all_gather.27
  29.2 5.4 all_gather.24
  38.5 25.0 %all-gather.7.cloned.1.call-done = bf16[2,1024,8,64]{1,3,2,0:T(8,128)(2,1)} async-done(((bf16[2,256,8,64]{1,3,2,0:T(8,128)(2,1)}), bf16[2,1024,8,64]{1,3,2,0:T(8,128)(2,1)}) %all-gather.7.cloned.1.call-update) | async-done | bytes 2097168 | tf_op jit(solution)/shard_map/all_gather | solution.py:228
  64.6 14.6 %while.58 = (s32[]{:T(128)}, f32[2,8,256]{2,1,0:T(8,128)S(1)}, f32[2,8,256]{2,1,0:T(8,128)S(1)}, f32[2,256,8,64]{1,3,2,0:T(8,128)}, s32[2]{0:T(128)S(1)}, /*inde...) while((s32[]{:T(128)}, f32[2,8,256]{2,1,0:T(8,128)S(1)}, ...), condition=%wide.region_5.6_spmd, body=%wide.region_0.5_spmd.sunk | while | flops 561132032 | bytes 48254400 | solution.py:66
  67.5 9.1 %conditional.4 = ((f32[2,8,256]{2,1,0:T(8,128)S(1)}, f32[2,8,256]{2,1,0:T(8,128)S(1)}, f32[2,256,8,64]{1,3,2,0:T(8,128)})) conditional(s32[]{:T(128)} %convert_element_type.296, (f32[2,8,256]{2,1,0:T(8,128)S(1)}, f32[2,8,256]{2,1,0:T(8,128)S(1)}, f32[2,256,8,64]{1,3,2,0:T(8,128)}) %tuple.147, (s32[2,256]{1,0:T(2,128)S(1)}, s32[]{:T(128)}, ...), branch_computations={%region_1.1_spmd, %region_2.4_spmd} | conditional | flops 561132032 | bytes 48254116 | solution.py:58
  88.5 24.9 %all-gather.11.cloned.1.call-done = bf16[2,1024,8,64]{1,3,2,0:T(8,128)(2,1)} async-done(((bf16[2,256,8,64]{1,3,2,0:T(8,128)(2,1)}), bf16[2,1024,8,64]{1,3,2,0:T(8,128)(2,1)}) %all-gather.11.cloned.1.call-update) | async-done | bytes 2097168 | tf_op jit(solution)/shard_map/all_gather | solution.py:247
  113.4 35.1 %while.60 = (s32[]{:T(128)}, f32[2,8,256]{2,1,0:T(8,128)S(1)}, f32[2,8,256]{2,1,0:T(8,128)S(1)}, f32[2,256,8,64]{1,3,2,0:T(8,128)}, s32[2,256]{1,0:T(2,128)S(1)}...) while((s32[]{:T(128)}, f32[2,8,256]{2,1,0:T(8,128)S(1)}, ...), condition=%wide.region_11.12_spmd.clone, body=%wide.region_8.11_spmd.clone.sunk | while | flops 561012736 | bytes 64764152 | solution.py:66
  114.8 6.0 fusion.222
  120.9 5.3 fusion.224
  132.1 6.0 fusion.222
  138.2 5.3 fusion.224
  144.0 4.3 fusion.226
  160.0 4.4 convert_reduce_fusion
  175.4 41.8 %while.61 = (s32[]{:T(128)}, f32[2,256,8,64]{1,3,2,0:T(8,128)}, f32[2,1024,8,64]{1,3,2,0:T(8,128)}, f32[2,1024,8,64]{1,3,2,0:T(8,128)}, s32[2]{0:T(128)S(1)}, /*...) while((s32[]{:T(128)}, f32[2,256,8,64]{1,3,2,0:T(8,128)}, ...), condition=%wide.region_22.23_spmd.clone, body=%wide.region_21.22_spmd.clone.sunk | while | flops 1365770240 | bytes 150796720 | solution.py:66
  187.0 4.5 fusion.240
  191.5 4.8 fusion.241
  199.3 4.2 fusion.238
  203.5 4.4 fusion.239
  208.0 4.5 fusion.240
  212.5 4.8 fusion.241
  231.8 46.2 %while.59 = (s32[]{:T(128)}, f32[2,256,8,64]{1,3,2,0:T(8,128)}, f32[2,1024,8,64]{1,3,2,0:T(8,128)}, f32[2,1024,8,64]{1,3,2,0:T(8,128)}, s32[2]{0:T(128)S(1)}, /*...) while((s32[]{:T(128)}, f32[2,256,8,64]{1,3,2,0:T(8,128)}, ...), condition=%wide.region_29.30_spmd, body=%wide.region_26.0_spmd.sunk | while | flops 1365901824 | bytes 121703928 | solution.py:66
  234.7 40.9 %conditional.5 = ((f32[2,256,8,64]{1,3,2,0:T(8,128)}, f32[2,1024,8,64]{1,3,2,0:T(8,128)}, f32[2,1024,8,64]{1,3,2,0:T(8,128)})) conditional(s32[]{:T(128)} %convert_element_type.297, (f32[2,256,8,64]{1,3,2,0:T(8,128)}, f32[2,1024,8,64]{1,3,2,0:T(8,128)}, f32[2,1024,8,64]{1,3,2,0:T(8,128)}) %tuple.150, (s32[2,256]{1,0:T(2,128)S(1)}, s32[]{:T(128)}, ...), branch_computations={%region_27.27_spmd, %region_28.28_spmd} | conditional | flops 1365901824 | bytes 121703600 | solution.py:58
  238.6 4.8 fusion.22
  248.6 10.5 %dynamic_update_slice.16 = f32[2,1024,8,64]{1,3,2,0:T(8,128)} dynamic-update-slice(f32[2,1024,8,64]{1,3,2,0:T(8,128)} %get-tuple-element.511, f32[2,512,8,64]{1,3,2,0:T(8,128)S(1)} %bitcast_add_fusion.1, s32[]{:T(128)} %constant.149.clone, s32[]{:T(128)S(6)} %select_n.62, s32[]{:T(128)} %constant.149.clone, s32[]{:T(128)} %constant.149.clone) | dynamic-update-slice | bytes 4194308 | tf_op jit(solution)/shard_map/while/body/eval_jaxpr/cond/branch_1_fun/dynamic_update_slice | solution.py:138
  259.0 6.1 bitcast_add_fusion
  265.1 10.4 %dynamic_update_slice.17 = f32[2,1024,8,64]{1,3,2,0:T(8,128)} dynamic-update-slice(f32[2,1024,8,64]{1,3,2,0:T(8,128)} %get-tuple-element.512, f32[2,512,8,64]{1,3,2,0:T(8,128)S(1)} %bitcast_add_fusion, s32[]{:T(128)} %constant.149.clone, s32[]{:T(128)S(6)} %select_n.62, s32[]{:T(128)} %constant.149.clone, s32[]{:T(128)} %constant.149.clone) | dynamic-update-slice | bytes 4194308 | tf_op jit(solution)/shard_map/while/body/eval_jaxpr/cond/branch_1_fun/dynamic_update_slice | solution.py:144
  312.9 39.3 %reduce-scatter.7.cloned.1.call-done = bf16[2,256,8,64]{1,3,2,0:T(8,128)(2,1)} async-done(((bf16[2,1024,8,64]{1,3,2,0:T(8,128)(2,1)}), bf16[2,256,8,64]{1,3,2,0:T(8,128)(2,1)}) %reduce-scatter.7.cloned.1.call-update) | async-done | bytes 524304 | tf_op jit(solution)/shard_map/reduce_scatter | solution.py:338
  353.4 33.3 %reduce-scatter.5.cloned.1.call-done = bf16[2,256,8,64]{1,3,2,0:T(8,128)(2,1)} async-done(((bf16[2,1024,8,64]{1,3,2,0:T(8,128)(2,1)}), bf16[2,256,8,64]{1,3,2,0:T(8,128)(2,1)}) %reduce-scatter.5.cloned.1.call-update) | async-done | bytes 524304 | tf_op jit(solution)/shard_map/reduce_scatter | solution.py:335
  388.0 32.7 %reduce-scatter.11.cloned.1.call-done = bf16[2,256,8,64]{1,3,2,0:T(8,128)(2,1)} async-done(((bf16[2,1024,8,64]{1,3,2,0:T(8,128)(2,1)}), bf16[2,256,8,64]{1,3,2,0:T(8,128)(2,1)}) %reduce-scatter.11.cloned.1.call-update) | async-done | bytes 524304 | tf_op jit(solution)/shard_map/reduce_scatter | solution.py:293
  422.0 32.9 %reduce-scatter.9.cloned.1.call-done = bf16[2,256,8,64]{1,3,2,0:T(8,128)(2,1)} async-done(((bf16[2,1024,8,64]{1,3,2,0:T(8,128)(2,1)}), bf16[2,256,8,64]{1,3,2,0:T(8,128)(2,1)}) %reduce-scatter.9.cloned.1.call-update) | async-done | bytes 524304 | tf_op jit(solution)/shard_map/reduce_scatter | solution.py:290
  464.4 42.6 %all-reduce = (f32[3,512]{1,0:T(4,128)}, f32[3,512]{1,0:T(4,128)}, f32[2048]{0:T(1024)}, f32[512]{0:T(512)}, f32[3,512]{1,0:T(4,128)}, /*index=5*/f32[3,512]{1,0:T(4,128)}) all-reduce(f32[3,512]{1,0:T(4,128)S(1)} %get-tuple-element.895, f32[3,512]{1,0:T(4,128)S(1)} %get-tuple-element.896, ...), channel_id=1, replica_groups=mesh['rows'=8,'seq'=4] {'rows','seq'}, use_global_device_ids=true, to_apply=%region_39.40 | all-reduce | flops 8704 | bytes 69632 | tf_op jit(solution)/shard_map/psum | solution.py:361
  513.9 234.3 %all-reduce.4.cloned.1.call-done = (f32[512,1536]{0,1:T(8,128)}, f32[512,512]{1,0:T(8,128)}, f32[512,512]{1,0:T(8,128)}, f32[512,1024]{0,1:T(8,128)}, f32[512,51...) async-done(((f32[512,1536]{0,1:T(8,128)}, f32[512,512]{1,0:T(8,128)}, f32[512,512]{1,0:T(8,128)}, f32[512,1024]{0,1:T(8,128)}, f32[512,512]{1,0:T(8,128)}, ...) | async-done | bytes 16777232 | tf_op jit(solution)/shard_map/psum | solution.py:361
  (383 shorter events, 180.3 us)
Async XLA Ops:
  7.2 146.7 %copy-start = (bf16[2048,512]{1,0:T(8,128)(2,1)S(1)}, bf16[2048,512]{1,0:T(8,128)(2,1)}, u32[]{:S(2)}) copy-start(bf16[2048,512]{1,0:T(8,128)(2,1)} %param.43) | copy-start | bytes 6291460
  7.2 31.3 %all-gather.5.cloned.1.call-start = ((), (), s32[]{:S(2)}) async-start(), calls=%async_computation.4 | async-start | bytes 2621440 | tf_op jit(solution)/shard_map/all_gather | solution.py:227
  12.7 50.8 %all-gather.7.cloned.1.call-start = ((), (), s32[]{:S(2)}) async-start(), calls=%async_computation.5 | async-start | bytes 2621440 | tf_op jit(solution)/shard_map/all_gather | solution.py:228
  15.6 72.9 %all-gather.9.cloned.1.call-start = ((), (), s32[]{:S(2)}) async-start(), calls=%async_computation.6 | async-start | bytes 2621440 | tf_op jit(solution)/shard_map/all_gather | solution.py:246
  19.1 10.1 %copy-start.52 = (s32[2,256]{1,0:T(2,128)S(1)}, s32[2,256]{1,0:T(2,128)}, u32[]{:S(2)}) copy-start(s32[2,256]{1,0:T(2,128)} %param.32) | copy-start | bytes 6148
  19.1 15.5 %copy-start.86 = (f32[3,512]{1,0:T(4,128)S(1)}, f32[3,512]{1,0:T(4,128)}, u32[]{:S(2)}) copy-start(f32[3,512]{1,0:T(4,128)} %param.46) | copy-start | bytes 18436
  19.1 15.5 %copy-start.87 = (f32[3,512]{1,0:T(4,128)S(1)}, f32[3,512]{1,0:T(4,128)}, u32[]{:S(2)}) copy-start(f32[3,512]{1,0:T(4,128)} %param.45) | copy-start | bytes 18436
  20.2 93.1 %all-gather.11.cloned.1.call-start = ((), (), s32[]{:S(2)}) async-start(), calls=%async_computation.7 | async-start | bytes 2621440 | tf_op jit(solution)/shard_map/all_gather | solution.py:247
  22.7 329.4 %reduce-scatter.7.cloned.1.call-start = ((), (), s32[]{:S(2)}) async-start(), calls=%async_computation.9 | async-start | bytes 2621440 | tf_op jit(solution)/shard_map/reduce_scatter | solution.py:338
  34.6 115.3 %copy-start.80 = (f32[1,512]{1,0:T(1,128)}, f32[1,512]{1,0:T(1,128)S(1)}, u32[]{:S(2)}) copy-start(f32[1,512]{1,0:T(1,128)S(1)} %get-tuple-element.875) | copy-start | bytes 6148
  34.6 119.2 %copy-start.71 = (f32[1,512]{1,0:T(1,128)}, f32[1,512]{1,0:T(1,128)S(1)}, u32[]{:S(2)}) copy-start(f32[1,512]{1,0:T(1,128)S(1)} %get-tuple-element.876) | copy-start | bytes 6148
  34.7 131.9 %copy-start.65 = (f32[1,512]{1,0:T(1,128)}, f32[1,512]{1,0:T(1,128)S(1)}, u32[]{:S(2)}) copy-start(f32[1,512]{1,0:T(1,128)S(1)} %get-tuple-element.873) | copy-start | bytes 6148
  64.6 16.2 %copy-start.36 = (bf16[512,512]{1,0:T(8,128)(2,1)S(1)}, bf16[512,512]{1,0:T(8,128)(2,1)}, u32[]{:S(2)}) copy-start(bf16[512,512]{1,0:T(8,128)(2,1)} %param.35) | copy-start | bytes 1572868
  82.8 30.5 %copy-start.75 = (f32[2,256]{1,0:T(2,128)}, f32[2,256]{1,0:T(2,128)S(1)}, u32[]{:S(2)}) copy-start(f32[2,256]{1,0:T(2,128)S(1)} %multiply_reduce_fusion.8) | copy-start | bytes 6148
  152.2 14.5 %copy-start.14 = (f32[2,256,512]{2,1,0:T(8,128)}, f32[2,256,512]{2,1,0:T(8,128)S(1)}, u32[]{:S(2)}) copy-start(f32[2,256,512]{2,1,0:T(8,128)S(1)} %get-tuple-element.888) | copy-start | bytes 3145732
  152.2 14.4 %copy-start.69 = (f32[2,256]{1,0:T(2,128)}, f32[2,256]{1,0:T(2,128)S(1)}, u32[]{:S(2)}) copy-start(f32[2,256]{1,0:T(2,128)S(1)} %broadcast_multiply_fusion.1) | copy-start | bytes 6148
  152.5 14.1 %copy-start.73 = (f32[2,256]{1,0:T(2,128)}, f32[2,256]{1,0:T(2,128)S(1)}, u32[]{:S(2)}) copy-start(f32[2,256]{1,0:T(2,128)S(1)} %fusion.148) | copy-start | bytes 6148
  281.9 104.8 %reduce-scatter.5.cloned.1.call-start = ((), (), s32[]{:S(2)}) async-start(), calls=%async_computation.8 | async-start | bytes 2621440 | tf_op jit(solution)/shard_map/reduce_scatter | solution.py:335
  285.9 134.9 %reduce-scatter.11.cloned.1.call-start = ((), (), s32[]{:S(2)}) async-start(), calls=%async_computation.11 | async-start | bytes 2621440 | tf_op jit(solution)/shard_map/reduce_scatter | solution.py:293
  289.8 165.1 %reduce-scatter.9.cloned.1.call-start = ((), (), s32[]{:S(2)}) async-start(), calls=%async_computation.10 | async-start | bytes 2621440 | tf_op jit(solution)/shard_map/reduce_scatter | solution.py:290
  293.8 9.8 %copy-start.13 = (f32[2,256,512]{2,1,0:T(8,128)S(1)}, f32[2,256,512]{2,1,0:T(8,128)}, u32[]{:S(2)}) copy-start(f32[2,256,512]{2,1,0:T(8,128)} %copy-done.11) | copy-start | bytes 3145732
  293.8 9.8 %copy-start.81 = (f32[1,512]{1,0:T(1,128)S(1)}, f32[1,512]{1,0:T(1,128)}, u32[]{:S(2)}) copy-start(f32[1,512]{1,0:T(1,128)} %copy-done.80) | copy-start | bytes 6148
  293.8 454.5 %all-reduce.4.cloned.1.call-start = ((), (), s32[]{:S(2)}) async-start(), calls=%async_computation.12 | async-start | bytes 33554432 | tf_op jit(solution)/shard_map/psum | solution.py:361
  312.9 144.1 %copy-start.55 = (bf16[2,256,512]{2,1,0:T(8,128)(2,1)S(1)}, bf16[2,256,512]{2,1,0:T(8,128)(2,1)}, u32[]{:S(2)}) copy-start(bf16[2,256,512]{2,1,0:T(8,128)(2,1)} %param.31) | copy-start | bytes 1572868
  312.9 147.2 %copy-start.38 = (bf16[2,256,512]{2,1,0:T(8,128)(2,1)S(1)}, bf16[2,256,512]{2,1,0:T(8,128)(2,1)}, u32[]{:S(2)}) copy-start(bf16[2,256,512]{2,1,0:T(8,128)(2,1)} %param.30) | copy-start | bytes 1572868
  312.9 147.2 %copy-start.56 = (bf16[2,256,512]{2,1,0:T(8,128)(2,1)S(1)}, bf16[2,256,512]{2,1,0:T(8,128)(2,1)}, u32[]{:S(2)}) copy-start(bf16[2,256,512]{2,1,0:T(8,128)(2,1)} %copy.89) | copy-start | bytes 1572868
  353.4 109.3 %copy-start.58 = (bf16[2,256,512]{2,1,0:T(8,128)(2,1)}, bf16[2,256,512]{2,1,0:T(8,128)(2,1)S(1)}, u32[]{:S(2)}) copy-start(bf16[2,256,512]{2,1,0:T(8,128)(2,1)S(1)} %copy.91) | copy-start | bytes 1572868
  388.0 74.8 %copy-start.59 = (bf16[2,256,512]{2,1,0:T(8,128)(2,1)}, bf16[2,256,512]{2,1,0:T(8,128)(2,1)S(1)}, u32[]{:S(2)}) copy-start(bf16[2,256,512]{2,1,0:T(8,128)(2,1)S(1)} %copy.90) | copy-start | bytes 1572868
  422.0 40.7 %copy-start.60 = (bf16[2,256,512]{2,1,0:T(8,128)(2,1)}, bf16[2,256,512]{2,1,0:T(8,128)(2,1)S(1)}, u32[]{:S(2)}) copy-start(bf16[2,256,512]{2,1,0:T(8,128)(2,1)S(1)} %copy.93) | copy-start | bytes 1572868
  462.9 44.2 %copy-start.50 = (bf16[512,1024]{1,0:T(8,128)(2,1)S(1)}, bf16[512,1024]{1,0:T(8,128)(2,1)}, u32[]{:S(2)}) copy-start(bf16[512,1024]{1,0:T(8,128)(2,1)} %param.38) | copy-start | bytes 3145732
  462.9 47.1 %copy-start.32 = (f32[2,256,512]{2,1,0:T(8,128)S(1)}, f32[2,256,512]{2,1,0:T(8,128)}, u32[]{:S(2)}) copy-start(f32[2,256,512]{2,1,0:T(8,128)} %copy-done.31) | copy-start | bytes 3145732
  464.0 46.0 %copy-start.57 = (bf16[2,256,512]{2,1,0:T(8,128)(2,1)S(1)}, bf16[2,256,512]{2,1,0:T(8,128)(2,1)}, u32[]{:S(2)}) copy-start(bf16[2,256,512]{2,1,0:T(8,128)(2,1)} %copy.89) | copy-start | bytes 1572868
  (81 other events, 319.3 us)
Sparse Core Ops, SparseCore 0:
  12.8 25.6 all-gather.4
  40.6 22.8 all-gather.6
  65.6 22.8 all-gather.8
  90.5 22.8 all-gather.10
  282.1 70.0 reduce-scatter.6
  355.3 31.4 reduce-scatter.4
  389.3 31.4 reduce-scatter.10
  423.4 31.4 reduce-scatter.8
  463.0 285.2 all-reduce.3
where the time goes:
time: 777 us; the launch traced here: 772 us
  waiting for transfers between devices  429 us (55%)
  matrix products  134 us (17%)
  local copies, waits for them, and re-layouts  80.6 us (10%)
  blocking collectives  54.2 us (7%)
  other arithmetic  49.1 us (6%)
  between operations  15.1 us (2%)
  loops' own time  9.55 us (1%)
    psum x1, waiting for transfers between devices, per_device(): lax.psum((d_self_qkv, d_self_out, d_self_bias, d_cross_q, d_cross_kv, d_c...  234 us
    psum x1, blocking collectives, per_device(): lax.psum((d_self_qkv, d_self_out, d_self_bias, d_cross_q, d_cross_kv, d_c...  42.6 us
    reduce_scatter x1, waiting for transfers between devices, per_device(): lax.psum_scatter(self_grads[2].astype(jnp.bfloat16), 'seq', scatter_dimen...  39.3 us
    reduce_scatter x1, waiting for transfers between devices, per_device(): lax.psum_scatter(self_grads[1].astype(jnp.bfloat16), 'seq', scatter_dimen...  33.3 us
    reduce_scatter x1, waiting for transfers between devices, per_device(): lax.psum_scatter(cross_grads[1].astype(jnp.bfloat16), 'seq', scatter_dime...  32.9 us
    reduce_scatter x1, waiting for transfers between devices, per_device(): lax.psum_scatter(cross_grads[2].astype(jnp.bfloat16), 'seq', scatter_dime...  32.7 us
    all_gather x1, waiting for transfers between devices, per_device(): lax.all_gather(value_rows, 'seq', axis=1, tiled=True)  25 us
    all_gather x1, waiting for transfers between devices, per_device(): lax.all_gather(cross_values, 'seq', axis=1, tiled=True)  24.9 us
  transfers between devices with their start and end apart: 9, of which 9 were waited for; matrix products, arithmetic and copies ran while one was open for 9% of the time, Pallas kernels for 0%

commit v1 on v0

v1 whole, which is shorter than its diff:
```python
import functools
import math

import jax
import jax.numpy as jnp
from jax import lax
from jax.experimental import pallas as pl
from jax.experimental.pallas import tpu as pltpu
from jax.sharding import PartitionSpec as P

HEADS = 8
PAIR = 128
EPS = 1e-05
SCALE = 0.125
NEG = -1e30
VMEM = 60 * 1024 * 1024
bf16 = jnp.bfloat16
f32 = jnp.float32


def params():
    return pltpu.CompilerParams(vmem_limit_bytes=VMEM)


def cost(flops, nbytes, trans=0):
    return pl.CostEstimate(flops=int(flops), bytes_accessed=int(nbytes), transcendentals=int(trans))


def dot(a, b):
    return jnp.dot(a, b, preferred_element_type=f32)


def dot_nt(a, b):
    return lax.dot_general(a, b, (((1,), (1,)), ((), ())), preferred_element_type=f32)


def dot_tn(a, b):
    return lax.dot_general(a, b, (((0,), (0,)), ((), ())), preferred_element_type=f32)


def col_sum(v):
    return jnp.sum(v.astype(f32), axis=0, keepdims=True)


def normalize(h):
    mean = jnp.mean(h, axis=-1, keepdims=True)
    c = h - mean
    r = lax.rsqrt(jnp.mean(c * c, axis=-1, keepdims=True) + EPS)
    return c * r, r


def norm_back(u, n, r, gain):
    w = u * gain
    return r * (
        w
        - jnp.mean(w, axis=-1, keepdims=True)
        - n * jnp.mean(w * n, axis=-1, keepdims=True)
    )


def whole(shape):
    return pl.BlockSpec(shape, lambda *_: (0,) * len(shape))


def smem():
    return pl.BlockSpec(memory_space=pltpu.SMEM)


def half_rows(g, which, count):
    at = g if which == 0 else 1 - g
    return pl.ds(pl.multiple_of(at * count, count), count)


class Plan:
    def __init__(self, dims, n, minimum=16):
        self.n, self.scatter, self.everywhere = n, [], []
        k = n
        for axis, base, m, at in dims:
            if m == 1:
                continue
            if not self.everywhere and k % m == 0 and k // m >= minimum:
                self.scatter.append((axis, base, m))
                k //= m
            else:
                self.everywhere.append((axis, base, m))
        self.k = k
        self.chunks = n // k
        place = 0
        for (axis, base, m), (_, _, _, at) in zip(self.scatter, [d for d in dims if d[2] > 1]):
            place = place * m + at
        self.place = place


def store_rel(ref, first, value, place, k, chunks):
    for w in range(value.shape[0] // k):
        at = jnp.bitwise_xor(place, first + w)
        ref[pl.ds(pl.multiple_of(at * k, k), k), :] = value[w * k : (w + 1) * k].astype(ref.dtype)


def swap(x, axis, off):
    size = lax.axis_size(axis)
    return lax.ppermute(x, axis, [(i, i ^ off) for i in range(size)])


def add_all(parts):
    total = parts[0].astype(f32)
    for part in parts[1:]:
        total = total + part.astype(f32)
    return total


def reduce_scatter(buf, plan):
    for axis, base, m in plan.scatter:
        k = buf.shape[0] // m
        parts = [buf[:k]]
        for j in range(1, m):
            parts.append(swap(buf[j * k : (j + 1) * k], axis, j * base))
        buf = add_all(parts).astype(buf.dtype)
    for axis, base, m in plan.everywhere:
        buf = add_all([buf] + [swap(buf, axis, j * base) for j in range(1, m)]).astype(buf.dtype)
    return buf


def all_gather(buf, plan):
    for axis, base, m in reversed(plan.scatter[1:]):
        buf = jnp.concatenate([buf] + [swap(buf, axis, j * base) for j in range(1, m)], axis=0)
    return buf, swap(buf, "seq", 1)


def unpack(name, sources, out_shape, out_map, blocks):
    size = 512
    scalars, operands, specs = [], [], []
    for own, other, plan in sources:
        scalars += [plan.place]
    table = {}
    for q, (src, b) in enumerate(blocks):
        table.setdefault(src, []).append((q, b))

    def rel_block(src, q, sc):
        plan = sources[src][2]
        entries = table[src]
        q0, b0 = entries[0]
        logical = jnp.clip(q - q0 + b0, b0, b0 + len(entries) - 1)
        return jnp.bitwise_xor(logical, sc[src] // (size // plan.k))

    for i, (own, other, plan) in enumerate(sources):
        nbh = own.shape[0] // size
        for arr in (own, other):
            operands.append(arr)
            specs.append(
                pl.BlockSpec(
                    (size, 512), lambda q, sc, i=i, nbh=nbh: (rel_block(i, q, sc) % nbh, 0)
                )
            )

    def kernel(sc, *refs):
        out = refs[-1]
        q = pl.program_id(0)
        for i, (own, other, plan) in enumerate(sources):
            nbh = own.shape[0] // size
            per = size // plan.k
            q0, q1 = table[i][0][0], table[i][-1][0]
            top = rel_block(i, q, sc) // nbh
            here = (q >= q0) & (q <= q1)
            for half in range(2):
                src = refs[2 * i + half]

                @pl.when(here & (top == half))
                def _():
                    low = sc[i] % per
                    for w in range(per):
                        at = jnp.bitwise_xor(low, w)
                        out[w * plan.k : (w + 1) * plan.k, :] = src[
                            pl.ds(pl.multiple_of(at * plan.k, plan.k), plan.k), :
                        ].astype(f32)

    return pl.pallas_call(
        kernel,
        grid_spec=pltpu.PrefetchScalarGridSpec(
            num_scalar_prefetch=1,
            grid=(len(blocks),),
            in_specs=specs,
            out_specs=pl.BlockSpec((size, 512), lambda q, sc: out_map(q)),
        ),
        out_shape=jax.ShapeDtypeStruct(out_shape, f32),
        compiler_params=params(),
        cost_estimate=cost(0, 6 * math.prod(out_shape)),
        name=name,
    )(jnp.stack(scalars).astype(jnp.int32), *operands)


def embed_kernel(parts, sc, tgt, recv, w, b, x_out, *outs):
    g = sc[0]
    tok = recv.shape[0]
    for which, x in ((0, tgt[g]), (1, recv[...])):
        rows = half_rows(g, which, tok)
        x_out[rows, :] = x
        y = dot(x, w[...]) + b[...]
        for i, (out, scale) in enumerate(zip(outs, parts)):
            piece = y[:, i * 512 : (i + 1) * 512]
            if scale != 1.0:
                piece = piece.astype(bf16).astype(f32) * scale
            out[rows, :] = piece.astype(bf16)


def embed(name, sc, local, recv, w, b, parts):
    tokens = 2 * recv.shape[0]
    one = jax.ShapeDtypeStruct((tokens, 512), bf16)
    vm = pl.BlockSpec(memory_space=pltpu.VMEM)
    return pl.pallas_call(
        functools.partial(embed_kernel, parts),
        in_specs=[smem()] + [vm] * 4,
        out_specs=[vm] * (1 + len(parts)),
        out_shape=[one] * (1 + len(parts)),
        compiler_params=params(),
        cost_estimate=cost(2 * tokens * 512 * w.shape[1], 4e6),
        name=name,
    )(sc, local, recv, w, b)


def row_to_cols(row):
    return jnp.transpose(jnp.broadcast_to(row, (PAIR, row.shape[1])))


def places(t, length, members, tok, shape, axis):
    at = lax.broadcasted_iota(jnp.int32, shape, axis)
    member = at // (2 * tok)
    inner = at - member * (2 * tok)
    low = jnp.bitwise_xor(member, t)
    block = jnp.where(inner < tok, low, 2 * members - 1 - low)
    return block * tok + jnp.where(inner < tok, inner, inner - tok)


def bias_of(causal, t, ids, tok, transposed):
    length = ids.shape[1]
    members = length // (2 * tok)
    q_row = ids[0:1, : 2 * tok]
    k_row = ids[0:1, :] if causal else ids[1:2, :]
    if transposed:
        allowed = row_to_cols(k_row)[:, 0:1] == q_row
        if causal:
            kp = places(t, length, members, tok, (length, 1), 0)
            qp = places(t, length, members, tok, (1, 2 * tok), 1)
            allowed = allowed & (kp <= qp)
    else:
        allowed = row_to_cols(q_row)[:, 0:1] == k_row
        if causal:
            kp = places(t, length, members, tok, (1, length), 1)
            qp = places(t, length, members, tok, (2 * tok, 1), 0)
            allowed = allowed & (kp <= qp)
    return jnp.where(allowed, 0.0, NEG).astype(f32)


def key_parts(own, others, tok):
    every = [own[...]] + [o[...] for o in others]
    low = jnp.concatenate([e[:tok] for e in every], axis=0)
    high = jnp.concatenate([e[tok:] for e in every], axis=0)
    return low, high


def bias_rows(bias, tok, members, half, transposed, cols):
    if transposed:
        return jnp.concatenate(
            [bias[(2 * j + half) * tok : (2 * j + half + 1) * tok, cols] for j in range(members)], axis=0
        )
    return jnp.concatenate(
        [bias[cols, (2 * j + half) * tok : (2 * j + half + 1) * tok] for j in range(members)], axis=1
    )


def lane_of_pair(shape):
    return lax.broadcasted_iota(jnp.int32, shape, 1) // 64


def attend_kernel(causal, tok, members, sc, ids, q, *refs):
    others = members - 1
    k_own, k_others = refs[0], refs[1 : 1 + others]
    v_own, v_others = refs[1 + others], refs[2 + others : 2 + 2 * others]
    out, lse, bias = refs[2 + 2 * others :]

    @pl.when(pl.program_id(0) == 0)
    def _():
        bias[...] = bias_of(causal, sc[1], ids[...], tok, False)

    k_low, k_high = key_parts(k_own, k_others, tok)
    v_low, v_high = key_parts(v_own, v_others, tok)
    k_all = jnp.concatenate([k_low, k_high], axis=0)
    v_all = jnp.concatenate([v_low, v_high], axis=0)
    lane = lane_of_pair((tok, PAIR))
    for b in range(2):
        rows = slice(b * tok, (b + 1) * tok)
        short = causal and b == 0
        kk, vv = (k_low, v_low) if short else (k_all, v_all)
        mask = bias_rows(bias, tok, members, 0, False, rows)
        if not short:
            mask = jnp.concatenate([mask, bias_rows(bias, tok, members, 1, False, rows)], axis=1)
        mixed, logs = [], []
        for h in range(2):
            qm = jnp.where(lane == h, q[rows, :], jnp.zeros((), bf16))
            s = dot_nt(qm, kk) + mask
            top = jnp.max(s, axis=-1, keepdims=True)
            p = jnp.exp(s - top)
            total = jnp.sum(p, axis=-1, keepdims=True)
            mixed.append(dot(p.astype(bf16), vv) / total)
            logs.append(top + jnp.log(total))
        out[rows, :] = jnp.where(lane == 0, mixed[0], mixed[1]).astype(bf16)
        both = jnp.transpose(jnp.where(lane == 0, logs[0], logs[1]))
        lse[0, 0:1, rows] = both[0:1]
        lse[0, 1:2, rows] = both[64:65]


def attend(name, causal, sc, ids, q, ks, vs):
    tokens = q.shape[0]
    length = ids.shape[1]
    members = len(ks)
    pair = pl.BlockSpec((tokens, PAIR), lambda p: (0, p))
    return pl.pallas_call(
        functools.partial(attend_kernel, causal, tokens // 2, members),
        grid=(4,),
        in_specs=[smem(), whole(ids.shape)] + [pair] * (1 + 2 * members),
        out_specs=[pair, pl.BlockSpec((1, 2, tokens), lambda p: (p, 0, 0))],
        out_shape=[
            jax.ShapeDtypeStruct((tokens, 512), bf16),
            jax.ShapeDtypeStruct((4, 2, tokens), f32),
        ],
        scratch_shapes=[pltpu.VMEM((tokens, length), f32)],
        compiler_params=params(),
        cost_estimate=cost(16 * tokens * length * 512, 4e6, 8 * tokens * length),
        name=name,
    )(sc, ids, q, *ks, *vs)


def attend_back_kernel(causal, tok, members, sc, ids, q, grad, lse, delta, *refs):
    others = members - 1
    k_own, k_others = refs[0], refs[1 : 1 + others]
    v_own, v_others = refs[1 + others], refs[2 + others : 2 + 2 * others]
    dq, dk, dv, bias = refs[2 + 2 * others :]

    @pl.when(pl.program_id(0) == 0)
    def _():
        bias[...] = bias_of(causal, sc[1], ids[...], tok, True)

    keys = key_parts(k_own, k_others, tok)
    values = key_parts(v_own, v_others, tok)
    lane = lane_of_pair((tok, PAIR))
    key_lane = lane_of_pair((tok * members, PAIR))
    grad_k, grad_v = [None, None], [None, None]

    def plus(total, term):
        return term if total is None else total + term

    for b in range(2):
        rows = slice(b * tok, (b + 1) * tok)
        grad_q = None
        for half in range(2):
            if causal and b == 0 and half == 1:
                continue
            kk, vv = keys[half], values[half]
            mask = bias_rows(bias, tok, members, half, True, rows)
            for h in range(2):
                qm = jnp.where(lane == h, q[rows, :], jnp.zeros((), bf16))
                gm = jnp.where(lane == h, grad[rows, :], jnp.zeros((), bf16))
                km = jnp.where(key_lane == h, kk, jnp.zeros((), bf16))
                p = jnp.exp(dot_nt(kk, qm) + mask - lse[0, h : h + 1, rows])
                ds = (p * (dot_nt(vv, gm) - delta[0, h : h + 1, rows])).astype(bf16)
                grad_v[half] = plus(grad_v[half], dot(p.astype(bf16), gm))
                grad_k[half] = plus(grad_k[half], dot(ds, qm))
                grad_q = plus(grad_q, dot_tn(ds, km))
        dq[rows, :] = (grad_q * SCALE).astype(bf16)
    for half in range(2):
        for j in range(members):
            to = slice((2 * j + half) * tok, (2 * j + half + 1) * tok)
            dk[to, :] = grad_k[half][j * tok : (j + 1) * tok].astype(bf16)
            dv[to, :] = grad_v[half][j * tok : (j + 1) * tok].astype(bf16)


def attend_back(name, causal, sc, ids, q, grad, lse, delta, ks, vs):
    tokens = q.shape[0]
    length = ids.shape[1]
    members = len(ks)
    pair = pl.BlockSpec((tokens, PAIR), lambda p: (0, p))
    row = pl.BlockSpec((1, 2, tokens), lambda p: (p, 0, 0))
    long = pl.BlockSpec((length, PAIR), lambda p: (0, p))
    return pl.pallas_call(
        functools.partial(attend_back_kernel, causal, tokens // 2, members),
        grid=(4,),
        in_specs=[smem(), whole(ids.shape), pair, pair, row, row] + [pair] * (2 * members),
        out_specs=[pair, long, long],
        out_shape=[
            jax.ShapeDtypeStruct((tokens, 512), bf16),
            jax.ShapeDtypeStruct((length, 512), bf16),
            jax.ShapeDtypeStruct((length, 512), bf16),
        ],
        scratch_shapes=[pltpu.VMEM((length, tokens), f32)],
        compiler_params=params(),
        cost_estimate=cost(40 * tokens * length * 512, 6e6, 8 * tokens * length),
        name=name,
    )(sc, ids, q, grad, lse, delta, *ks, *vs)


def after_self_kernel(x, mixed, w_out, sbias, gain, shift, w_q, cbias, n0, r0, q2):
    h = x[...].astype(f32) + dot(mixed[...], w_out[...]) + sbias[2:3, :]
    n, r = normalize(h)
    n0[...] = n
    r0[...] = r
    first = n * gain[0:1, :] + shift[0:1, :]
    q = dot(first.astype(bf16), w_q[...]) + cbias[0:1, :]
    q2[...] = (q.astype(bf16).astype(f32) * SCALE).astype(bf16)


def after_self(x, mixed, w_out, sbias, gain, shift, w_q, cbias):
    tokens = x.shape[0]
    vm = pl.BlockSpec(memory_space=pltpu.VMEM)
    return pl.pallas_call(
        after_self_kernel,
        in_specs=[vm] * 8,
        out_specs=[vm] * 3,
        out_shape=[
            jax.ShapeDtypeStruct((tokens, 512), f32),
            jax.ShapeDtypeStruct((tokens, 1), f32),
            jax.ShapeDtypeStruct((tokens, 512), bf16),
        ],
        compiler_params=params(),
        cost_estimate=cost(4 * tokens * 512 * 512, 4e6),
        name="after_self",
    )(x, mixed, w_out, sbias, gain, shift, w_q, cbias)


def head_sums(a, b):
    prod = a * b
    high = prod.astype(bf16)
    low = (prod - high.astype(f32)).astype(bf16)
    pick = (
        lax.broadcasted_iota(jnp.int32, (HEADS, 512), 1) // 64
        == lax.broadcasted_iota(jnp.int32, (HEADS, 512), 0)
    ).astype(bf16)
    return dot_nt(pick, high) + dot_nt(pick, low)


def put_head_rows(ref, rows):
    for p in range(4):
        ref[p] = rows[2 * p : 2 * p + 2]


def gelu_parts(v):
    c = math.sqrt(2.0 / math.pi)
    v2 = v * v
    t = jnp.tanh(c * v * (1.0 + 0.044715 * v2))
    half = 0.5 * (1.0 + t)
    slope = half + 0.5 * v * (1.0 - t * t) * (c * (1.0 + 3.0 * 0.044715 * v2))
    return v * half, slope


def mid_kernel(
    chunks, k_in, k_out, sc, n0, mixed, cout, cbias, gain, shift, w_in, b_in, w_out, b_out, cot,
    cot_recv, own_out, send_out, d_in, d_out, d_cout, small, grad_two, grad_mixed, delta,
    inner, slope, low, n1, r1, total, grad_three, outer,
):
    i = pl.program_id(0)
    g = sc[0]
    tok = cot_recv.shape[0]

    @pl.when(i == 0)
    def _():
        first = n0[...] * gain[0:1, :] + shift[0:1, :]
        n, r = normalize(first + dot(mixed[...], cout[...]) + cbias[2:3, :])
        n1[...] = n
        r1[...] = r
        second = n * gain[1:2, :] + shift[1:2, :]
        low[...] = second.astype(bf16)
        total[...] = second + b_out[...]
        small[...] = jnp.zeros_like(small)

    @pl.when(i < chunks)
    def _():
        pre = dot(low[...], w_in[...]) + b_in[...]
        act, grad_act = gelu_parts(pre)
        act = act.astype(bf16)
        inner[i] = act
        slope[i] = grad_act.astype(bf16)
        total[...] += dot(act, w_out[...])

    @pl.when(i == chunks - 1)
    def _():
        n, r = normalize(total[...])
        result = n * gain[2:3, :] + shift[2:3, :]
        total[...] = result
        own_out[...] = total[half_rows(g, 0, tok), :]
        send_out[...] = total[half_rows(g, 1, tok), :].astype(bf16)
        total[half_rows(g, 0, tok), :] = cot[g].astype(f32)
        total[half_rows(g, 1, tok), :] = cot_recv[...].astype(f32)
        u = total[...]
        small[0:1, :] = col_sum(u * n)
        small[1:2, :] = col_sum(u)
        back = norm_back(u, n, r, gain[2:3, :])
        grad_three[...] = back
        back_low = back.astype(bf16)
        outer[...] = back_low
        small[2:3, :] = col_sum(back_low)
        total[...] = back

    @pl.when(i >= chunks)
    def _():
        j = i - chunks
        back = dot_nt(outer[...], w_out[...]) * slope[j].astype(f32)
        pre_low = back.astype(bf16)
        small[pl.ds(8 + j, 1), :] = col_sum(pre_low)
        per = 512 // k_in
        store_rel(d_in, 0, dot_tn(low[...], pre_low), sc[2] % per, k_in, per)
        per = 512 // k_out
        store_rel(d_out, 0, dot_tn(inner[j], outer[...]), sc[3] % per, k_out, per)
        total[...] += dot_nt(pre_low, w_in[...])

    @pl.when(i == 2 * chunks - 1)
    def _():
        u = total[...]
        n = n1[...]
        small[3:4, :] = col_sum(u * n)
        small[4:5, :] = col_sum(u)
        back = norm_back(u, n, r1[...], gain[1:2, :])
        grad_two[...] = back
        back_low = back.astype(bf16)
        small[5:6, :] = col_sum(back_low)
        d_cout[...] = dot_tn(mixed[...], back_low).astype(bf16)
        g_mixed = dot_nt(back_low, cout[...]).astype(bf16)
        grad_mixed[...] = g_mixed
        put_head_rows(delta, head_sums(g_mixed.astype(f32), mixed[...].astype(f32)))


def middle(sc, plan_in, plan_out, n0, mixed, cout, cbias, gain, shift, w_in, b_in, w_out, b_out, cot, cot_recv):
    tokens = n0.shape[0]
    tok = tokens // 2
    ff = w_in.shape[1]
    chunks = ff // 512
    sds = jax.ShapeDtypeStruct

    def rel(plan, which):
        per = 512 // plan.k
        return pl.BlockSpec(
            (512, 512),
            lambda i, sc: (jnp.bitwise_xor(jnp.maximum(i - chunks, 0), sc[which] // per), 0),
        )

    return pl.pallas_call(
        functools.partial(mid_kernel, chunks, plan_in.k, plan_out.k),
        grid_spec=pltpu.PrefetchScalarGridSpec(
            num_scalar_prefetch=1,
            grid=(2 * chunks,),
            in_specs=[
                whole((tokens, 512)),
                whole((tokens, 512)),
                whole((512, 512)),
                whole((3, 512)),
                whole((3, 512)),
                whole((3, 512)),
                pl.BlockSpec((512, 512), lambda i, sc: (0, i % chunks)),
                pl.BlockSpec((1, 512), lambda i, sc: (0, i % chunks)),
                pl.BlockSpec((512, 512), lambda i, sc: (i % chunks, 0)),
                whole((1, 512)),
                whole(cot.shape),
                whole(cot_recv.shape),
            ],
            out_specs=[
                whole((tok, 512)),
                whole((tok, 512)),
                rel(plan_in, 2),
                rel(plan_out, 3),
                whole((512, 512)),
                whole((8 + chunks + 4, 512)),
                whole((tokens, 512)),
                whole((tokens, 512)),
                whole((4, 2, tokens)),
            ],
            scratch_shapes=[
                pltpu.VMEM((chunks, tokens, 512), bf16),
                pltpu.VMEM((chunks, tokens, 512), bf16),
                pltpu.VMEM((tokens, 512), bf16),
                pltpu.VMEM((tokens, 512), f32),
                pltpu.VMEM((tokens, 1), f32),
                pltpu.VMEM((tokens, 512), f32),
                pltpu.VMEM((tokens, 512), f32),
                pltpu.VMEM((tokens, 512), bf16),
            ],
        ),
        out_shape=[
            sds((tok, 512), f32),
            sds((tok, 512), bf16),
            sds((ff, 512), bf16),
            sds((ff, 512), bf16),
            sds((512, 512), bf16),
            sds((8 + chunks + 4, 512), f32),
            sds((tokens, 512), f32),
            sds((tokens, 512), bf16),
            sds((4, 2, tokens), f32),
        ],
        compiler_params=params(),
        cost_estimate=cost(2 * tokens * 512 * (6 * ff + 3 * 512), 2e7),
        name="middle",
    )(sc, n0, mixed, cout, cbias, gain, shift, w_in, b_in, w_out, b_out, cot, cot_recv)


def after_cross_kernel(
    k, chunks, sc, dq, grad_two, n0, r0, w_q, mixed, w_out, gain, shift, d_cout,
    buf, d_sout, small, grad_one, grad_mixed, delta,
):
    place = sc[4]
    n = n0[...]
    first = (n * gain[0:1, :] + shift[0:1, :]).astype(bf16)
    half = 512 // k
    store_rel(buf, 0, d_cout[...], place, k, chunks)
    store_rel(buf, half, dot_tn(first, dq[...]), place, k, chunks)
    u = grad_two[...] + dot_nt(dq[...], w_q[...])
    small[...] = jnp.zeros_like(small)
    small[0:1, :] = col_sum(u * n)
    small[1:2, :] = col_sum(u)
    small[2:3, :] = col_sum(dq[...])
    back = norm_back(u, n, r0[...], gain[0:1, :])
    grad_one[...] = back
    back_low = back.astype(bf16)
    small[3:4, :] = col_sum(back_low)
    d_sout[...] = dot_tn(mixed[...], back_low).astype(bf16)
    g_mixed = dot_nt(back_low, w_out[...]).astype(bf16)
    grad_mixed[...] = g_mixed
    put_head_rows(delta, head_sums(g_mixed.astype(f32), mixed[...].astype(f32)))


def after_cross(sc, plan, dq, grad_two, n0, r0, w_q, mixed, w_out, gain, shift, d_cout):
    tokens = dq.shape[0]
    sds = jax.ShapeDtypeStruct
    vm = pl.BlockSpec(memory_space=pltpu.VMEM)
    return pl.pallas_call(
        functools.partial(after_cross_kernel, plan.k, plan.chunks),
        in_specs=[smem()] + [vm] * 10,
        out_specs=[vm] * 6,
        out_shape=[
            sds((1024, 512), bf16),
            sds((512, 512), bf16),
            sds((8, 512), f32),
            sds((tokens, 512), f32),
            sds((tokens, 512), bf16),
            sds((4, 2, tokens), f32),
        ],
        compiler_params=params(),
        cost_estimate=cost(8 * tokens * 512 * 512, 6e6),
        name="after_cross",
    )(sc, dq, grad_two, n0, r0, w_q, mixed, w_out, gain, shift, d_cout)


def sum_parts(own, others, tokens):
    total = own[:tokens].astype(f32)
    for o in others:
        total = total + o[...].astype(f32)
    return total.astype(bf16)


def memory_grad_kernel(n_other, k, chunks, sc, x, w, *refs):
    dk = sum_parts(refs[0], refs[1 : 1 + n_other], x.shape[0])
    dv = sum_parts(refs[1 + n_other], refs[2 + n_other : 2 + 2 * n_other], x.shape[0])
    own_out, send_out, buf, small, total = refs[2 + 2 * n_other :]
    tok = own_out.shape[0]
    g, place = sc[0], sc[5]
    per = 512 // k
    store_rel(buf, 0, dot_tn(x[...], dk), place, k, chunks)
    store_rel(buf, per, dot_tn(x[...], dv), place, k, chunks)
    small[...] = jnp.zeros_like(small)
    small[0:1, :] = col_sum(dv)
    total[...] = dot_nt(dk, w[:, :512]) + dot_nt(dv, w[:, 512:])
    own_out[...] = total[half_rows(g, 0, tok), :]
    send_out[...] = total[half_rows(g, 1, tok), :].astype(bf16)


def memory_grad(sc, plan, x, w, dks, dvs):
    tokens = x.shape[0]
    tok = tokens // 2
    sds = jax.ShapeDtypeStruct
    vm = pl.BlockSpec(memory_space=pltpu.VMEM)
    n_other = len(dks) - 1
    keys = [vm] * (1 + n_other)
    return pl.pallas_call(
        functools.partial(memory_grad_kernel, n_other, plan.k, plan.chunks),
        in_specs=[smem(), vm, vm] + keys + keys,
        out_specs=[vm] * 4,
        out_shape=[
            sds((tok, 512), f32),
            sds((tok, 512), bf16),
            sds((1024, 512), bf16),
            sds((8, 512), f32),
        ],
        scratch_shapes=[pltpu.VMEM((tokens, 512), f32)],
        compiler_params=params(),
        cost_estimate=cost(8 * tokens * 512 * 512, 6e6),
        name="memory_grad",
    )(sc, x, w, *dks, *dvs)


def target_grad_kernel(n_other, ka, ca, kb, cb, sc, x, w, grad_one, dq, d_sout, *refs):
    dk = sum_parts(refs[0], refs[1 : 1 + n_other], x.shape[0])
    dv = sum_parts(refs[1 + n_other], refs[2 + n_other : 2 + 2 * n_other], x.shape[0])
    own_out, send_out, buf_a, buf_b, small, total = refs[2 + 2 * n_other :]
    tok = own_out.shape[0]
    g = sc[0]
    store_rel(buf_a, 0, dot_tn(x[...], dq[...]), sc[6], ka, ca)
    store_rel(buf_a, 512 // ka, dot_tn(x[...], dk), sc[6], ka, ca)
    store_rel(buf_b, 0, dot_tn(x[...], dv), sc[7], kb, cb)
    store_rel(buf_b, 512 // kb, d_sout[...], sc[7], kb, cb)
    small[...] = jnp.zeros_like(small)
    small[0:1, :] = col_sum(dq[...])
    small[1:2, :] = col_sum(dv)
    total[...] = (
        grad_one[...]
        + dot_nt(dq[...], w[:, :512])
        + dot_nt(dk, w[:, 512:1024])
        + dot_nt(dv, w[:, 1024:])
    )
    own_out[...] = total[half_rows(g, 0, tok), :]
    send_out[...] = total[half_rows(g, 1, tok), :].astype(bf16)


def target_grad(sc, plan_a, plan_b, x, w, grad_one, dq, d_sout, dks, dvs):
    tokens = x.shape[0]
    tok = tokens // 2
    sds = jax.ShapeDtypeStruct
    vm = pl.BlockSpec(memory_space=pltpu.VMEM)
    n_other = len(dks) - 1
    keys = [vm] * (1 + n_other)
    return pl.pallas_call(
        functools.partial(target_grad_kernel, n_other, plan_a.k, plan_a.chunks, plan_b.k, plan_b.chunks),
        in_specs=[smem()] + [vm] * 5 + keys + keys,
        out_specs=[vm] * 5,
        out_shape=[
            sds((tok, 512), f32),
            sds((tok, 512), bf16),
            sds((1024, 512), bf16),
            sds((1024, 512), bf16),
            sds((8, 512), f32),
        ],
        scratch_shapes=[pltpu.VMEM((tokens, 512), f32)],
        compiler_params=params(),
        cost_estimate=cost(12 * tokens * 512 * 512, 8e6),
        name="target_grad",
    )(sc, x, w, grad_one, dq, d_sout, *dks, *dvs)


def per_device(
    target, memory, tgt_group, src_group, self_qkv, self_out, self_bias, cross_q, cross_kv, cross_out,
    cross_bias, ffn_in, ffn_in_bias, ffn_out, ffn_out_bias, norm_gain, norm_bias, cotangent,
):
    rows_here, tok, width = target.shape
    ff = ffn_in.shape[1]
    seq, rows = lax.axis_size("seq"), lax.axis_size("rows")
    members = seq // 2
    s, r = lax.axis_index("seq"), lax.axis_index("rows")
    g = s // members
    t = jnp.where(g == 0, s, seq - 1 - s)

    dim_c = ("seq", 1, 2, s % 2)
    dim_x = ("seq", 2, seq // 2, s // 2)
    dim_y = ("rows", 1, 2, r % 2)
    dim_z = ("rows", 2, rows // 2, r // 2)
    order_a = [dim_c, dim_x, dim_y, dim_z]
    order_b = [dim_c, dim_y, dim_x, dim_z]
    ffa, ffb = Plan(order_a, ff), Plan(order_b, ff)
    pa, pb = Plan(order_a, 1024), Plan(order_b, 1024)
    sc = jnp.stack([g, t, ffa.place, ffb.place, pb.place, pa.place, pa.place, pb.place]).astype(jnp.int32)

    def partner(x):
        return swap(x, "seq", seq - 1)

    def others_of(x):
        return [swap(x, "seq", j) for j in range(1, members)]

    def pick(x, which):
        return lax.dynamic_index_in_dim(x, g if which == 0 else 1 - g, 0, keepdims=False)

    def home(own, back):
        back = back.astype(f32)
        return jnp.where(g == 0, jnp.stack([own, back]), jnp.stack([back, own]))

    ids = jnp.stack([tgt_group, src_group]).astype(f32)
    ids_own = lax.dynamic_index_in_dim(ids, g, 1, keepdims=False)
    ids_recv = partner(lax.dynamic_index_in_dim(ids, 1 - g, 1, keepdims=False))
    tgt_recv = partner(pick(target, 1))
    mem_recv = partner(pick(memory, 1))
    cot_recv = partner(pick(cotangent, 1))
    ids_here = jnp.concatenate(
        [jnp.where(g == 0, ids_own, ids_recv), jnp.where(g == 0, ids_recv, ids_own)], axis=1
    )
    ids_all = jnp.concatenate([ids_here] + others_of(ids_here), axis=1)

    zero = jnp.zeros((width,), f32)
    qkv_bias = jnp.concatenate([self_bias[0], zero, self_bias[1]])[None]
    kv_bias = jnp.concatenate([zero, cross_bias[1]])[None]
    x, q1, k1, v1 = embed("embed_target", sc, target, tgt_recv, self_qkv, qkv_bias, (SCALE, 1.0, 1.0))
    k1s, v1s = [k1] + others_of(k1), [v1] + others_of(v1)
    xm, k2, v2 = embed("embed_memory", sc, memory, mem_recv, cross_kv, kv_bias, (1.0, 1.0))
    k2s, v2s = [k2] + others_of(k2), [v2] + others_of(v2)

    mixed1, lse1 = attend("self_attend", True, sc, ids_all, q1, k1s, v1s)
    n0, r0, q2 = after_self(x, mixed1, self_out, self_bias, norm_gain, norm_bias, cross_q, cross_bias)
    mixed2, lse2 = attend("cross_attend", False, sc, ids_all, q2, k2s, v2s)
    own_y, send_y, d_in, d_out, d_cout, small_mid, grad_two, grad_mixed2, delta2 = middle(
        sc, ffa, ffb, n0, mixed2, cross_out, cross_bias, norm_gain, norm_bias, ffn_in, ffn_in_bias[None],
        ffn_out, ffn_out_bias[None], cotangent, cot_recv,
    )
    layer_out = home(own_y, partner(send_y))

    red_in, red_out = reduce_scatter(d_in, ffa), reduce_scatter(d_out, ffb)
    got_in, got_out = all_gather(red_in, ffa), all_gather(red_out, ffb)
    nb = ff // 512
    d_ffn_in = unpack(
        "unpack_in", [(*got_in, ffa)], (512, ff), lambda q: (0, q), [(0, b) for b in range(nb)]
    )
    d_ffn_out = unpack(
        "unpack_out", [(*got_out, ffb)], (ff, 512), lambda q: (q, 0), [(0, b) for b in range(nb)]
    )

    dq2, dk2, dv2 = attend_back("cross_back", False, sc, ids_all, q2, grad_mixed2, lse2, delta2, k2s, v2s)

    def home_parts(d):
        tokens = 2 * tok
        return [d] + [swap(d[j * tokens : (j + 1) * tokens], "seq", j) for j in range(1, members)]

    buf_b, d_sout, small_cross, grad_one, grad_mixed1, delta1 = after_cross(
        sc, pb, dq2, grad_two, n0, r0, cross_q, mixed1, self_out, norm_gain, norm_bias, d_cout
    )
    own_m, send_m, buf_a, small_mem = memory_grad(sc, pa, xm, cross_kv, home_parts(dk2), home_parts(dv2))
    d_memory = home(own_m, partner(send_m))
    got_a = all_gather(reduce_scatter(buf_a, pa), pa)
    got_b = all_gather(reduce_scatter(buf_b, pb), pb)
    d_cross_kv = unpack("unpack_kv", [(*got_a, pa)], (512, 1024), lambda q: (0, q), [(0, 0), (0, 1)])
    d_cross_out = unpack("unpack_co", [(*got_b, pb)], (512, 512), lambda q: (0, 0), [(0, 0)])
    d_cross_q = unpack("unpack_cq", [(*got_b, pb)], (512, 512), lambda q: (0, 0), [(0, 1)])

    dq1, dk1, dv1 = attend_back("self_back", True, sc, ids_all, q1, grad_mixed1, lse1, delta1, k1s, v1s)
    own_t, send_t, buf_c, buf_d, small_tgt = target_grad(
        sc, pa, pb, x, self_qkv, grad_one, dq1, d_sout, home_parts(dk1), home_parts(dv1)
    )
    d_target = home(own_t, partner(send_t))
    got_c = all_gather(reduce_scatter(buf_c, pa), pa)
    got_d = all_gather(reduce_scatter(buf_d, pb), pb)
    d_self_qkv = unpack(
        "unpack_qkv", [(*got_c, pa), (*got_d, pb)], (512, 1536), lambda q: (0, q), [(0, 0), (0, 1), (1, 0)]
    )
    d_self_out = unpack("unpack_so", [(*got_d, pb)], (512, 512), lambda q: (0, 0), [(0, 1)])

    small = jnp.concatenate([small_mid, small_cross, small_mem, small_tgt], axis=0)
    for axis, base, m, _ in order_a:
        if m > 1:
            small = add_all([small] + [swap(small, axis, j * base) for j in range(1, m)])
    mid = small_mid.shape[0]
    crs, mem, tg = small[mid:], small[mid + 8 :], small[mid + 16 :]
    d_self_bias = jnp.stack([tg[0], tg[1], crs[3]])
    d_cross_bias = jnp.stack([crs[2], mem[0], small[5]])
    d_ffn_in_bias = small[8 : 8 + nb].reshape(ff)
    d_norm_gain = jnp.stack([crs[0], small[3], small[0]])
    d_norm_bias = jnp.stack([crs[1], small[4], small[1]])
    return (
        layer_out, d_target, d_memory, d_self_qkv, d_self_out, d_self_bias, d_cross_q, d_cross_kv,
        d_cross_out, d_cross_bias, d_ffn_in, d_ffn_in_bias, d_ffn_out, small[2], d_norm_gain, d_norm_bias,
    )


def solution(mesh):
    sharded, ids, copied = P("rows", "seq", None), P("rows", "seq"), P()
    in_specs = (sharded, sharded, ids, ids) + (copied,) * 13 + (sharded,)
    out_specs = (sharded,) * 3 + (copied,) * 13
    return jax.shard_map(per_device, mesh=mesh, in_specs=in_specs, out_specs=out_specs, check_vma=False)
```

time: 777 us -> 348 us (0.45)
  waiting for transfers between devices: 429 us -> 105 us
  matrix products: 134 us -> 0 us
  Pallas kernels: 0 us -> 119 us
  starting transfers between devices: 0.54 us -> 78.4 us
  blocking collectives: 54.2 us -> 0 us
  local copies, waits for them, and re-layouts: 80.6 us -> 29.5 us
  other arithmetic: 49.1 us -> 11.2 us
  between operations: 15.1 us -> 2.01 us
  loops' own time: 9.55 us -> 0 us
    psum x1 -> x0, waiting for transfers between devices: 234 us -> none  [per_device(): lax.psum((d_self_qkv, d_self_out, d_self_bias, d_cross_q, d_cross_kv, d_c...]
    reduce_scatter x4 -> x0, waiting for transfers between devices: 138 us -> none  [the longest x1 39.3 us: per_device(): lax.psum_scatter(self_grads[2].astype(jnp.bfloat16), 'seq', scatter_dimen...]
    dot_general x42 -> x0, matrix products: 134 us -> none  [the longest x6 21.4 us: compute(): jnp.einsum('rqhd,rkhd->rhqk', queries, key_block, preferred_element_type=...]
    pallas_call x0 -> x18, Pallas kernels: none -> 119 us  [the longest x2 28.1 us: attend_back(): pl.pallas_call(functools.partial(attend_back_kernel, causal, tokens // 2,...]
    ppermute x0 -> x94, waiting for transfers between devices: none -> 105 us  [swap(): return lax.ppermute(x, axis, [(i, i ^ off) for i in range(size)])]
    ppermute x0 -> x94, starting transfers between devices: none -> 78.4 us  [swap(): return lax.ppermute(x, axis, [(i, i ^ off) for i in range(size)])]
    all_gather x4 -> x0, waiting for transfers between devices: 56.1 us -> none  [the longest x1 25 us: per_device(): lax.all_gather(value_rows, 'seq', axis=1, tiled=True)]
    psum x1 -> x0, blocking collectives: 42.6 us -> none  [per_device(): lax.psum((d_self_qkv, d_self_out, d_self_bias, d_cross_q, d_cross_kv, d_c...]
  transfers between devices with their start and end apart: 9 -> 94, of which waited for: 9 -> 42; matrix products, arithmetic and copies ran while one was open for 9% -> 9% of each run, Pallas kernels for 0% -> 23%
where the time goes in v1:
time: 348 us; the launch traced here: 344 us
  Pallas kernels  119 us (34%)
  waiting for transfers between devices  105 us (30%)
  starting transfers between devices  78.4 us (23%)
  local copies, waits for them, and re-layouts  29.5 us (8%)
  other arithmetic  11.2 us (3%)
    ppermute x94, waiting for transfers between devices, swap(): return lax.ppermute(x, axis, [(i, i ^ off) for i in range(size)])  105 us
    ppermute x94, starting transfers between devices, swap(): return lax.ppermute(x, axis, [(i, i ^ off) for i in range(size)])  78.4 us
    pallas_call x2, Pallas kernels, attend_back(): pl.pallas_call(functools.partial(attend_back_kernel, causal, tokens // 2,...  28.1 us
    pallas_call x7, Pallas kernels, unpack(): pl.pallas_call(kernel, grid_spec=pltpu.PrefetchScalarGridSpec(num_scalar_...  23.1 us
    pallas_call x2, Pallas kernels, attend(): pl.pallas_call(functools.partial(attend_kernel, causal, tokens // 2, memb...  21.4 us
    pallas_call x1, Pallas kernels, middle(): pl.pallas_call(functools.partial(mid_kernel, chunks, plan_in.k, plan_out....  19.4 us
    unnamed x92, local copies, waits for them, and re-layouts  9.62 us
    slice x4, local copies, waits for them, and re-layouts, home_parts(): d[j * tokens:(j + 1) * tokens]  7.86 us
  transfers between devices with their start and end apart: 94, of which 42 were waited for; matrix products, arithmetic and copies ran while one was open for 9% of the time, Pallas kernels for 23%

profile of v1, /device:TPU:0, one launch (start us, length us, event | category | flops | bytes accessed | tf_op | source)
XLA Modules:
  0.0 344.5 jit_solution(14875767653161453663)
XLA Ops:
  11.6 3.5 %embed_target.1 = (bf16[512,512]{1,0:T(8,128)(2,1)}, bf16[512,512]{1,0:T(8,128)(2,1)}, bf16[512,512]{1,0:T(8,128)(2,1)}, bf16[512,512]{1,0:T(8,128)(2,1)}) custom-call(s32[8]{0:T(128)} %stack.107.sc, bf16[2,256,512]{2,1,0:T(8,128)(2,1)} %tgt.2, bf16[256,512]{1,0:T(8,128)(2,1)} %copy-done.27, bf16[512,1536]{1,0:T(8,128)(2,1)} %w.6, f32[1,1536]{1,0:T(1,128)} %broadcast_in_dim.16.b), custom_call_target="tpu_custom_call" | custom-call | flops 805306368 | bytes 4000000 | tf_op jit(solution)/shard_map/embed_target/pallas_call | solution.py:210
  20.4 3.1 embed_memory.1
  25.5 10.4 %self_attend.1 = (bf16[512,512]{1,0:T(8,128)(2,1)}, f32[4,2,512]{2,1,0:T(2,128)}) custom-call(s32[8]{0:T(128)} %stack.107.sc, f32[2,1024]{1,0:T(2,128)} %pad_maximum_fusion.7.ids, bf16[512,512]{1,0:T(8,128)(2,1)} %get-tuple-element.61.q, bf16[512,512]{1,0:T(8,128)(2,1)} %get-tuple-element.62.refs_0_, bf16[512,512]{1,0:T(8,128)(2,1)} %copy-done.21, ...), custom_call_target="tpu_custom_call" | custom-call | flops 4294967296 | bytes 4000000 | tf_op jit(solution)/shard_map/self_attend/pallas_call | solution.py:317
  35.9 3.6 %after_self.1 = (f32[512,512]{1,0:T(8,128)}, f32[512,1]{1,0:T(8,128)}, bf16[512,512]{1,0:T(8,128)(2,1)}) custom-call(bf16[512,512]{1,0:T(8,128)(2,1)} %get-tuple-element.60.x, bf16[512,512]{1,0:T(8,128)(2,1)} %get-tuple-element.64.mixed, bf16[512,512]{1,0:T(8,128)(2,1)} %w_out.5, f32[3,512]{1,0:T(4,128)} %sbias.1, f32[3,512]{1,0:T(4,128)} %gain.5, ...), custom_call_target="tpu_custom_call" | custom-call | flops 536870912 | bytes 4000000 | tf_op jit(solution)/shard_map/after_self/pallas_call | solution.py:414
  40.5 11.0 %cross_attend.1 = (bf16[512,512]{1,0:T(8,128)(2,1)}, f32[4,2,512]{2,1,0:T(2,128)}) custom-call(s32[8]{0:T(128)} %stack.107.sc, f32[2,1024]{1,0:T(2,128)} %pad_maximum_fusion.7.ids, bf16[512,512]{1,0:T(8,128)(2,1)} %get-tuple-element.66.q, bf16[512,512]{1,0:T(8,128)(2,1)} %get-tuple-element.67.refs_0_, bf16[512,512]{1,0:T(8,128)(2,1)} %copy-done.23, ...), custom_call_target="tpu_custom_call" | custom-call | flops 4294967296 | bytes 4000000 | tf_op jit(solution)/shard_map/cross_attend/pallas_call | solution.py:317
  52.2 19.4 %middle.1 = (f32[256,512]{1,0:T(8,128)}, bf16[256,512]{1,0:T(8,128)(2,1)}, bf16[2048,512]{1,0:T(8,128)(2,1)}, bf16[2048,512]{1,0:T(8,128)(2,1)}, bf16[512,512]{1...) custom-call(s32[8]{0:T(128)} %stack.107.sc, ...), custom_call_target="tpu_custom_call" | custom-call | flops 7247757312 | bytes 20000000 | tf_op jit(solution)/shard_map/middle/pallas_call | solution.py:544
  71.6 15.4 %cross_back.1 = (bf16[512,512]{1,0:T(8,128)(2,1)}, bf16[1024,512]{1,0:T(8,128)(2,1)}, bf16[1024,512]{1,0:T(8,128)(2,1)}) custom-call(s32[8]{0:T(128)} %stack.107.sc, f32[2,1024]{1,0:T(2,128)} %pad_maximum_fusion.7.ids, bf16[512,512]{1,0:T(8,128)(2,1)} %get-tuple-element.66.q, bf16[512,512]{1,0:T(8,128)(2,1)} %get-tuple-element.72.grad, ...), custom_call_target="tpu_custom_call" | custom-call | flops 10737418240 | bytes 6000000 | tf_op jit(solution)/shard_map/cross_back/pallas_call | solution.py:384
  91.3 5.3 %after_cross.1 = (bf16[1024,512]{1,0:T(8,128)(2,1)}, bf16[512,512]{1,0:T(8,128)(2,1)}, f32[8,512]{1,0:T(8,128)}, f32[512,512]{1,0:T(8,128)}, bf16[512,512]{1,0:T(8,128)(2,1)}, /*index=5*/f32[4,2,512]{2,1,0:T(2,128)}) custom-call(s32[8]{0:T(128)} %stack.107.sc, bf16[512,512]{1,0:T(8,128)(2,1)} %get-tuple-element.75.dq, ...), custom_call_target="tpu_custom_call" | custom-call | flops 1073741824 | bytes 6000000 | tf_op jit(solution)/shard_map/after_cross/pallas_call | solution.py:631
  96.6 12.7 %self_back.1 = (bf16[512,512]{1,0:T(8,128)(2,1)}, bf16[1024,512]{1,0:T(8,128)(2,1)}, bf16[1024,512]{1,0:T(8,128)(2,1)}) custom-call(s32[8]{0:T(128)} %stack.107.sc, f32[2,1024]{1,0:T(2,128)} %pad_maximum_fusion.7.ids, bf16[512,512]{1,0:T(8,128)(2,1)} %get-tuple-element.61.q, bf16[512,512]{1,0:T(8,128)(2,1)} %get-tuple-element.80.grad, ...), custom_call_target="tpu_custom_call" | custom-call | flops 10737418240 | bytes 6000000 | tf_op jit(solution)/shard_map/self_back/pallas_call | solution.py:384
  118.5 4.9 %memory_grad.1 = (f32[256,512]{1,0:T(8,128)}, bf16[256,512]{1,0:T(8,128)(2,1)}, bf16[1024,512]{1,0:T(8,128)(2,1)}, f32[8,512]{1,0:T(8,128)}) custom-call(s32[8]{0:T(128)} %stack.107.sc, bf16[512,512]{1,0:T(8,128)(2,1)} %get-tuple-element.89.x, bf16[512,1024]{1,0:T(8,128)(2,1)} %w.7, bf16[1024,512]{1,0:T(8,128)(2,1)} %get-tuple-element.90.refs_0_, ...), custom_call_target="tpu_custom_call" | custom-call | flops 1073741824 | bytes 6000000 | tf_op jit(solution)/shard_map/memory_grad/pallas_call | solution.py:679
  124.3 6.5 %target_grad.1 = (f32[256,512]{1,0:T(8,128)}, bf16[256,512]{1,0:T(8,128)(2,1)}, bf16[1024,512]{1,0:T(8,128)(2,1)}, bf16[1024,512]{1,0:T(8,128)(2,1)}, f32[8,512]{1,0:T(8,128)}) custom-call(s32[8]{0:T(128)} %stack.107.sc, bf16[512,512]{1,0:T(8,128)(2,1)} %get-tuple-element.60.x, bf16[512,1536]{1,0:T(8,128)(2,1)} %w.6, f32[512,512]{1,0:T(8,128)} %get-tuple-element.79.grad_one, ...), custom_call_target="tpu_custom_call" | custom-call | flops 1610612736 | bytes 8000000 | tf_op jit(solution)/shard_map/target_grad/pallas_call | solution.py:726
  136.8 2.8 collective-permute-done.41
  146.6 5.3 %collective-permute-done.12 = bf16[256,512]{1,0:T(8,128)(2,1)S(1)} collective-permute-done((bf16[256,512]{1,0:T(8,128)(2,1)S(1)}, bf16[256,512]{1,0:T(8,128)(2,1)S(1)}, u32[]{:S(2)}, u32[]{:S(2)}) %collective-permute-start.12) | collective-permute-done | bytes 262176 | tf_op jit(solution)/shard_map/ppermute | solution.py:102
  157.2 2.6 collective-permute-start.50
  162.3 3.2 collective-permute-done.51
  165.7 3.9 %collective-permute-done.52 = bf16[32,512]{1,0:T(8,128)(2,1)S(1)} collective-permute-done((bf16[32,512]{1,0:T(8,128)(2,1)S(1)}, bf16[32,512]{1,0:T(8,128)(2,1)S(1)}, u32[]{:S(2)}, u32[]{:S(2)}) %collective-permute-start.52) | collective-permute-done | bytes 32800 | tf_op jit(solution)/shard_map/ppermute | solution.py:102
  169.6 5.2 %collective-permute-done.53 = bf16[32,512]{1,0:T(8,128)(2,1)S(1)} collective-permute-done((bf16[32,512]{1,0:T(8,128)(2,1)S(1)}, bf16[32,512]{1,0:T(8,128)(2,1)S(1)}, u32[]{:S(2)}, u32[]{:S(2)}) %collective-permute-start.53) | collective-permute-done | bytes 32800 | tf_op jit(solution)/shard_map/ppermute | solution.py:102
  174.7 5.7 %collective-permute-done.54 = bf16[32,512]{1,0:T(8,128)(2,1)S(1)} collective-permute-done((bf16[32,512]{1,0:T(8,128)(2,1)S(1)}, bf16[32,512]{1,0:T(8,128)(2,1)S(1)}, u32[]{:S(2)}, u32[]{:S(2)}) %collective-permute-start.54) | collective-permute-done | bytes 32800 | tf_op jit(solution)/shard_map/ppermute | solution.py:102
  188.5 5.6 %collective-permute-done.59 = bf16[256,512]{1,0:T(8,128)(2,1)S(1)} collective-permute-done((bf16[256,512]{1,0:T(8,128)(2,1)S(1)}, bf16[256,512]{1,0:T(8,128)(2,1)S(1)}, u32[]{:S(2)}, u32[]{:S(2)}) %collective-permute-start.59) | collective-permute-done | bytes 262176 | tf_op jit(solution)/shard_map/ppermute | solution.py:102
  195.1 7.9 %collective-permute-done.29 = bf16[256,512]{1,0:T(8,128)(2,1)S(1)} collective-permute-done((bf16[256,512]{1,0:T(8,128)(2,1)S(1)}, bf16[256,512]{1,0:T(8,128)(2,1)S(1)}, u32[]{:S(2)}, u32[]{:S(2)}) %collective-permute-start.29) | collective-permute-done | bytes 262176 | tf_op jit(solution)/shard_map/ppermute | solution.py:102
  231.2 2.6 collective-permute-start.66
  236.9 2.9 collective-permute-start.36
  253.1 4.8 %collective-permute-done.84 = bf16[256,512]{1,0:T(8,128)(2,1)S(1)} collective-permute-done((bf16[256,512]{1,0:T(8,128)(2,1)S(1)}, bf16[256,512]{1,0:T(8,128)(2,1)S(1)}, u32[]{:S(2)}, u32[]{:S(2)}) %collective-permute-start.84) | collective-permute-done | bytes 262176 | tf_op jit(solution)/shard_map/ppermute | solution.py:102
  270.3 3.9 %collective-permute-done.74 = bf16[64,512]{1,0:T(8,128)(2,1)S(1)} collective-permute-done((bf16[64,512]{1,0:T(8,128)(2,1)S(1)}, bf16[64,512]{1,0:T(8,128)(2,1)S(1)}, u32[]{:S(2)}, u32[]{:S(2)}) %collective-permute-start.74) | collective-permute-done | bytes 65568 | tf_op jit(solution)/shard_map/ppermute | solution.py:102
  281.6 2.9 collective-permute-done.77
  289.1 4.9 %collective-permute-done.91 = bf16[256,512]{1,0:T(8,128)(2,1)S(1)} collective-permute-done((bf16[256,512]{1,0:T(8,128)(2,1)S(1)}, bf16[256,512]{1,0:T(8,128)(2,1)S(1)}, u32[]{:S(2)}, u32[]{:S(2)}) %collective-permute-start.91) | collective-permute-done | bytes 262176 | tf_op jit(solution)/shard_map/ppermute | solution.py:102
  298.0 6.7 %collective-permute-done.25 = bf16[128,512]{1,0:T(8,128)(2,1)S(1)} collective-permute-done((bf16[128,512]{1,0:T(8,128)(2,1)S(1)}, bf16[128,512]{1,0:T(8,128)(2,1)S(1)}, u32[]{:S(2)}, u32[]{:S(2)}) %collective-permute-start.25) | collective-permute-done | bytes 131104 | tf_op jit(solution)/shard_map/ppermute | solution.py:102
  311.7 5.3 %collective-permute-done.38 = bf16[256,512]{1,0:T(8,128)(2,1)S(1)} collective-permute-done((bf16[256,512]{1,0:T(8,128)(2,1)S(1)}, bf16[256,512]{1,0:T(8,128)(2,1)S(1)}, u32[]{:S(2)}, u32[]{:S(2)}) %collective-permute-start.38) | collective-permute-done | bytes 262176 | tf_op jit(solution)/shard_map/ppermute | solution.py:102
  324.8 2.6 unpack_kv.1
  330.5 4.3 %unpack_qkv.1 = f32[512,1536]{1,0:T(8,128)} custom-call(s32[2]{0:T(128)} %pad_add_fusion.sc, bf16[512,512]{1,0:T(8,128)(2,1)} %copy-done.13, bf16[512,512]{1,0:T(8,128)(2,1)} %collective-permute-done.27.refs_1_, bf16[512,512]{1,0:T(8,128)(2,1)} %copy-done.1, bf16[512,512]{1,0:T(8,128)(2,1)} %copy-done.6), custom_call_target="tpu_custom_call" | custom-call | bytes 4718592 | tf_op jit(solution)/shard_map/unpack_qkv/pallas_call | solution.py:177
  334.8 4.7 %unpack_out.1 = f32[2048,512]{1,0:T(8,128)} custom-call(s32[1]{0:T(128)} %bitcast.3.sc, bf16[1024,512]{1,0:T(8,128)(2,1)} %copy-done.7, bf16[1024,512]{1,0:T(8,128)(2,1)} %collective-permute-done.93.refs_1_), custom_call_target="tpu_custom_call" | custom-call | bytes 6291456 | tf_op jit(solution)/shard_map/unpack_out/pallas_call | solution.py:177
  339.5 4.7 %unpack_in.1 = f32[512,2048]{1,0:T(8,128)} custom-call(s32[1]{0:T(128)} %bitcast.2.sc, bf16[1024,512]{1,0:T(8,128)(2,1)} %constant_dynamic-update-slice_fusion.53.refs_0_, bf16[1024,512]{1,0:T(8,128)(2,1)} %collective-permute-done.81.refs_1_), custom_call_target="tpu_custom_call" | custom-call | bytes 6291456 | tf_op jit(solution)/shard_map/unpack_in/pallas_call | solution.py:177
  (367 shorter events, 154.1 us)
Async XLA Ops:
  4.9 14.3 %collective-permute-start.1 = (f32[2,256]{1,0:T(2,128)S(1)}, f32[2,256]{1,0:T(2,128)S(1)}, u32[]{:S(2)}, u32[]{:S(2)}) collective-permute-start(f32[2,256]{1,0:T(2,128)S(1)} %bitcast.49), channel_id=1, source_target_pairs={{0,3},{1,2},{2,1},{3,0},{4,7},{5,6},{6,5},{7,4},{8,11},{9,10},{10,... | collective-permute-start | bytes 6152 | tf_op jit(solution)/shard_map/ppermute | solution.py:102
  5.9 13.7 %collective-permute-start.5 = (bf16[256,512]{1,0:T(8,128)(2,1)S(1)}, bf16[256,512]{1,0:T(8,128)(2,1)S(1)}, u32[]{:S(2)}, u32[]{:S(2)}) collective-permute-start(bf16[256,512]{1,0:T(8,128)(2,1)S(1)} %dynamic-slice_bitcast_fusion.1), channel_id=1, source_target_pairs={{0,3},{1,2},{2,1},{3,0},{4,7},{5,6},{6,5},{7,4},{8,11},{9,10},{10,... | collective-permute-start | bytes 786440 | tf_op jit(solution)/shard_map/ppermute | solution.py:102
  16.2 35.2 %collective-permute-start.8 = (bf16[256,512]{1,0:T(8,128)(2,1)S(1)}, bf16[256,512]{1,0:T(8,128)(2,1)S(1)}, u32[]{:S(2)}, u32[]{:S(2)}) collective-permute-start(bf16[256,512]{1,0:T(8,128)(2,1)S(1)} %dynamic-slice_bitcast_fusion), channel_id=1, source_target_pairs={{0,3},{1,2},{2,1},{3,0},{4,7},{5,6},{6,5},{7,4},{8,11},{9,10},{10,... | collective-permute-start | bytes 786440 | tf_op jit(solution)/shard_map/ppermute | solution.py:102
  23.4 16.1 %collective-permute-start.6 = (bf16[512,512]{1,0:T(8,128)(2,1)}, bf16[512,512]{1,0:T(8,128)(2,1)S(1)}, u32[]{:S(2)}, u32[]{:S(2)}) collective-permute-start(bf16[512,512]{1,0:T(8,128)(2,1)} %get-tuple-element.67.refs_0_), channel_id=1, source_target_pairs={{0,1},{1,0},{2,3},{3,2},{4,5},{5,4},{6,7},{7,6},{8,9},{9,8},{10,11... | collective-permute-start | bytes 1572872 | tf_op jit(solution)/shard_map/ppermute | solution.py:102
  23.6 15.9 %collective-permute-start.7 = (bf16[512,512]{1,0:T(8,128)(2,1)}, bf16[512,512]{1,0:T(8,128)(2,1)S(1)}, u32[]{:S(2)}, u32[]{:S(2)}) collective-permute-start(bf16[512,512]{1,0:T(8,128)(2,1)} %get-tuple-element.68.refs_2_), channel_id=1, source_target_pairs={{0,1},{1,0},{2,3},{3,2},{4,5},{5,4},{6,7},{7,6},{8,9},{9,8},{10,11... | collective-permute-start | bytes 1572872 | tf_op jit(solution)/shard_map/ppermute | solution.py:102
  88.9 28.7 %collective-permute-start.13 = (bf16[512,512]{1,0:T(8,128)(2,1)}, bf16[512,512]{1,0:T(8,128)(2,1)S(1)}, u32[]{:S(2)}, u32[]{:S(2)}) collective-permute-start(bf16[512,512]{1,0:T(8,128)(2,1)} %slice.257), channel_id=1, source_target_pairs={{0,1},{1,0},{2,3},{3,2},{4,5},{5,4},{6,7},{7,6},{8,9},{9,8},{10,11... | collective-permute-start | bytes 1572872 | tf_op jit(solution)/shard_map/ppermute | solution.py:102
  91.0 27.0 %collective-permute-start.14 = (bf16[512,512]{1,0:T(8,128)(2,1)}, bf16[512,512]{1,0:T(8,128)(2,1)}, u32[]{:S(2)}, u32[]{:S(2)}) collective-permute-start(bf16[512,512]{1,0:T(8,128)(2,1)} %slice.258), channel_id=1, source_target_pairs={{0,1},{1,0},{2,3},{3,2},{4,5},{5,4},{6,7},{7,6},{8,9},{9,8},{10,11... | collective-permute-start | bytes 1572872 | tf_op jit(solution)/shard_map/ppermute | solution.py:102
  111.4 12.7 %collective-permute-start.10 = (bf16[512,512]{1,0:T(8,128)(2,1)}, bf16[512,512]{1,0:T(8,128)(2,1)}, u32[]{:S(2)}, u32[]{:S(2)}) collective-permute-start(bf16[512,512]{1,0:T(8,128)(2,1)} %slice.255), channel_id=1, source_target_pairs={{0,1},{1,0},{2,3},{3,2},{4,5},{5,4},{6,7},{7,6},{8,9},{9,8},{10,11... | collective-permute-start | bytes 1572872 | tf_op jit(solution)/shard_map/ppermute | solution.py:102
  113.6 10.7 %collective-permute-start.11 = (bf16[512,512]{1,0:T(8,128)(2,1)}, bf16[512,512]{1,0:T(8,128)(2,1)}, u32[]{:S(2)}, u32[]{:S(2)}) collective-permute-start(bf16[512,512]{1,0:T(8,128)(2,1)} %slice.256), channel_id=1, source_target_pairs={{0,1},{1,0},{2,3},{3,2},{4,5},{5,4},{6,7},{7,6},{8,9},{9,8},{10,11... | collective-permute-start | bytes 1572872 | tf_op jit(solution)/shard_map/ppermute | solution.py:102
  115.4 16.7 %collective-permute-start.46 = (bf16[512,512]{1,0:T(8,128)(2,1)}, bf16[512,512]{1,0:T(8,128)(2,1)}, u32[]{:S(2)}, u32[]{:S(2)}) collective-permute-start(bf16[512,512]{1,0:T(8,128)(2,1)} %slice.282), channel_id=1, source_target_pairs={{0,1},{1,0},{2,3},{3,2},{4,5},{5,4},{6,7},{7,6},{8,9},{9,8},{10,11... | collective-permute-start | bytes 1572872 | tf_op jit(solution)/shard_map/ppermute | solution.py:102
  117.6 62.8 %collective-permute-start.82 = (bf16[1024,512]{1,0:T(8,128)(2,1)}, bf16[1024,512]{1,0:T(8,128)(2,1)}, u32[]{:S(2)}, u32[]{:S(2)}) collective-permute-start(bf16[1024,512]{1,0:T(8,128)(2,1)} %slice.316), channel_id=1, source_target_pairs={{0,1},{1,0},{2,3},{3,2},{4,5},{5,4},{6,7},{7,6},{8,9},{9,8},{10,11... | collective-permute-start | bytes 3145736 | tf_op jit(solution)/shard_map/ppermute | solution.py:102
  118.0 64.1 %collective-permute-start.70 = (bf16[1024,512]{1,0:T(8,128)(2,1)}, bf16[1024,512]{1,0:T(8,128)(2,1)S(1)}, u32[]{:S(2)}, u32[]{:S(2)}) collective-permute-start(bf16[1024,512]{1,0:T(8,128)(2,1)} %slice.305), channel_id=1, source_target_pairs={{0,1},{1,0},{2,3},{3,2},{4,5},{5,4},{6,7},{7,6},{8,9},{9,8},{10,11... | collective-permute-start | bytes 3145736 | tf_op jit(solution)/shard_map/ppermute | solution.py:102
  124.1 12.5 %collective-permute-start.9 = (bf16[256,512]{1,0:T(8,128)(2,1)S(1)}, bf16[256,512]{1,0:T(8,128)(2,1)S(1)}, u32[]{:S(2)}, u32[]{:S(2)}) collective-permute-start(bf16[256,512]{1,0:T(8,128)(2,1)S(1)} %copy-done.25), channel_id=1, source_target_pairs={{0,3},{1,2},{2,1},{3,0},{4,7},{5,6},{6,5},{7,4},{8,11},{9,10},{10,... | collective-permute-start | bytes 786440 | tf_op jit(solution)/shard_map/ppermute | solution.py:102
  133.4 10.7 %collective-permute-start.47 = (bf16[256,512]{1,0:T(8,128)(2,1)S(1)}, bf16[256,512]{1,0:T(8,128)(2,1)S(1)}, u32[]{:S(2)}, u32[]{:S(2)}) collective-permute-start(bf16[256,512]{1,0:T(8,128)(2,1)S(1)} %slice.351), channel_id=1, source_target_pairs={{0,4},{4,0},{8,12},{12,8},{16,20},{20,16},{24,28},{28,24},{1,5},{5... | collective-permute-start | bytes 786440 | tf_op jit(solution)/shard_map/ppermute | solution.py:102
  144.3 11.2 %collective-permute-start.48 = (bf16[128,512]{1,0:T(8,128)(2,1)S(1)}, bf16[128,512]{1,0:T(8,128)(2,1)S(1)}, u32[]{:S(2)}, u32[]{:S(2)}) collective-permute-start(bf16[128,512]{1,0:T(8,128)(2,1)S(1)} %slice.353), channel_id=1, source_target_pairs={{0,2},{1,3},{2,0},{3,1},{4,6},{5,7},{6,4},{7,5},{8,10},{9,11},{10,... | collective-permute-start | bytes 393224 | tf_op jit(solution)/shard_map/ppermute | solution.py:102
  161.1 21.4 %collective-permute-start.58 = (bf16[512,512]{1,0:T(8,128)(2,1)S(1)}, bf16[512,512]{1,0:T(8,128)(2,1)S(1)}, u32[]{:S(2)}, u32[]{:S(2)}) collective-permute-start(bf16[512,512]{1,0:T(8,128)(2,1)S(1)} %slice.292), channel_id=1, source_target_pairs={{0,1},{1,0},{2,3},{3,2},{4,5},{5,4},{6,7},{7,6},{8,9},{9,8},{10,11... | collective-permute-start | bytes 1572872 | tf_op jit(solution)/shard_map/ppermute | solution.py:102
  162.3 21.7 %collective-permute-start.28 = (bf16[512,512]{1,0:T(8,128)(2,1)S(1)}, bf16[512,512]{1,0:T(8,128)(2,1)S(1)}, u32[]{:S(2)}, u32[]{:S(2)}) collective-permute-start(bf16[512,512]{1,0:T(8,128)(2,1)S(1)} %slice.270), channel_id=1, source_target_pairs={{0,1},{1,0},{2,3},{3,2},{4,5},{5,4},{6,7},{7,6},{8,9},{9,8},{10,11... | collective-permute-start | bytes 1572872 | tf_op jit(solution)/shard_map/ppermute | solution.py:102
  180.5 127.9 %collective-permute-start.43 = (f32[40,512]{1,0:T(8,128)S(1)}, f32[40,512]{1,0:T(8,128)S(1)}, u32[]{:S(2)}, u32[]{:S(2)}) collective-permute-start(f32[40,512]{1,0:T(8,128)S(1)} %add.197), channel_id=1, source_target_pairs={{0,8},{4,12},{8,0},{12,4},{16,24},{20,28},{24,16},{28,20},{1,9},{5... | collective-permute-start | bytes 245768 | tf_op jit(solution)/shard_map/ppermute | solution.py:102
  182.6 68.7 %collective-permute-start.83 = (bf16[512,512]{1,0:T(8,128)(2,1)S(1)}, bf16[512,512]{1,0:T(8,128)(2,1)S(1)}, u32[]{:S(2)}, u32[]{:S(2)}) collective-permute-start(bf16[512,512]{1,0:T(8,128)(2,1)S(1)} %slice.379), channel_id=1, source_target_pairs={{0,4},{4,0},{8,12},{12,8},{16,20},{20,16},{24,28},{28,24},{1,5},{5... | collective-permute-start | bytes 1572872 | tf_op jit(solution)/shard_map/ppermute | solution.py:102
  185.9 17.1 %collective-permute-start.29 = (bf16[256,512]{1,0:T(8,128)(2,1)S(1)}, bf16[256,512]{1,0:T(8,128)(2,1)S(1)}, u32[]{:S(2)}, u32[]{:S(2)}) collective-permute-start(bf16[256,512]{1,0:T(8,128)(2,1)S(1)} %slice.341), channel_id=1, source_target_pairs={{0,4},{4,0},{8,12},{12,8},{16,20},{20,16},{24,28},{28,24},{1,5},{5... | collective-permute-start | bytes 786440 | tf_op jit(solution)/shard_map/ppermute | solution.py:102
  188.5 15.8 %collective-permute-start.17 = (bf16[256,512]{1,0:T(8,128)(2,1)S(1)}, bf16[256,512]{1,0:T(8,128)(2,1)S(1)}, u32[]{:S(2)}, u32[]{:S(2)}) collective-permute-start(bf16[256,512]{1,0:T(8,128)(2,1)S(1)} %slice.333), channel_id=1, source_target_pairs={{0,2},{1,3},{2,0},{3,1},{4,6},{5,7},{6,4},{7,5},{8,10},{9,11},{10,... | collective-permute-start | bytes 786440 | tf_op jit(solution)/shard_map/ppermute | solution.py:102
  194.1 14.5 %collective-permute-start.56 = (bf16[256,512]{1,0:T(8,128)(2,1)S(1)}, bf16[256,512]{1,0:T(8,128)(2,1)S(1)}, u32[]{:S(2)}, u32[]{:S(2)}) collective-permute-start(bf16[256,512]{1,0:T(8,128)(2,1)S(1)} %get-tuple-element.131), channel_id=1, source_target_pairs={{0,4},{4,0},{8,12},{12,8},{16,20},{20,16},{24,28},{28,24},{1,5},{5... | collective-permute-start | bytes 786440 | tf_op jit(solution)/shard_map/ppermute | solution.py:102
  239.9 12.1 %collective-permute-start.71 = (bf16[512,512]{1,0:T(8,128)(2,1)S(1)}, bf16[512,512]{1,0:T(8,128)(2,1)S(1)}, u32[]{:S(2)}, u32[]{:S(2)}) collective-permute-start(bf16[512,512]{1,0:T(8,128)(2,1)S(1)} %slice.370), channel_id=1, source_target_pairs={{0,2},{1,3},{2,0},{3,1},{4,6},{5,7},{6,4},{7,5},{8,10},{9,11},{10,... | collective-permute-start | bytes 1572872 | tf_op jit(solution)/shard_map/ppermute | solution.py:102
  247.5 48.9 %collective-permute-start.67 = (bf16[128,512]{1,0:T(8,128)(2,1)S(1)}, bf16[128,512]{1,0:T(8,128)(2,1)S(1)}, u32[]{:S(2)}, u32[]{:S(2)}) collective-permute-start(bf16[128,512]{1,0:T(8,128)(2,1)S(1)} %pad_maximum_fusion.5), channel_id=1, source_target_pairs={{0,4},{4,0},{8,12},{12,8},{16,20},{20,16},{24,28},{28,24},{1,5},{5... | collective-permute-start | bytes 393224 | tf_op jit(solution)/shard_map/ppermute | solution.py:102
  281.6 15.5 %collective-permute-start.37 = (bf16[128,512]{1,0:T(8,128)(2,1)S(1)}, bf16[128,512]{1,0:T(8,128)(2,1)S(1)}, u32[]{:S(2)}, u32[]{:S(2)}) collective-permute-start(bf16[128,512]{1,0:T(8,128)(2,1)S(1)} %pad_maximum_fusion.3), channel_id=1, source_target_pairs={{0,2},{1,3},{2,0},{3,1},{4,6},{5,7},{6,4},{7,5},{8,10},{9,11},{10,... | collective-permute-start | bytes 393224 | tf_op jit(solution)/shard_map/ppermute | solution.py:102
  294.1 10.7 %collective-permute-start.92 = (bf16[512,512]{1,0:T(8,128)(2,1)S(1)}, bf16[512,512]{1,0:T(8,128)(2,1)S(1)}, u32[]{:S(2)}, u32[]{:S(2)}) collective-permute-start(bf16[512,512]{1,0:T(8,128)(2,1)S(1)} %get-tuple-element.116), channel_id=1, source_target_pairs={{0,4},{4,0},{8,12},{12,8},{16,20},{20,16},{24,28},{28,24},{1,5},{5... | collective-permute-start | bytes 1572872 | tf_op jit(solution)/shard_map/ppermute | solution.py:102
  295.2 12.0 %collective-permute-start.80 = (bf16[512,512]{1,0:T(8,128)(2,1)S(1)}, bf16[512,512]{1,0:T(8,128)(2,1)S(1)}, u32[]{:S(2)}, u32[]{:S(2)}) collective-permute-start(bf16[512,512]{1,0:T(8,128)(2,1)S(1)} %get-tuple-element.121), channel_id=1, source_target_pairs={{0,2},{1,3},{2,0},{3,1},{4,6},{5,7},{6,4},{7,5},{8,10},{9,11},{10,... | collective-permute-start | bytes 1572872 | tf_op jit(solution)/shard_map/ppermute | solution.py:102
  297.0 11.9 %collective-permute-start.44 = (f32[40,512]{1,0:T(8,128)S(1)}, f32[40,512]{1,0:T(8,128)S(1)}, u32[]{:S(2)}, u32[]{:S(2)}) collective-permute-start(f32[40,512]{1,0:T(8,128)S(1)} %add.197), channel_id=1, source_target_pairs={{0,16},{4,20},{8,24},{12,28},{16,0},{20,4},{24,8},{28,12},{1,17},{... | collective-permute-start | bytes 245768 | tf_op jit(solution)/shard_map/ppermute | solution.py:102
  307.2 10.3 %collective-permute-start.57 = (bf16[512,512]{1,0:T(8,128)(2,1)S(1)}, bf16[512,512]{1,0:T(8,128)(2,1)S(1)}, u32[]{:S(2)}, u32[]{:S(2)}) collective-permute-start(bf16[512,512]{1,0:T(8,128)(2,1)S(1)} %constant_dynamic-update-slice_fusion.31.refs_0_), channel_id=1, source_target_pairs={{0,1},{1,0},{2,3},{3,2},{4,5},{5,4},{6,7},{7,6},{8,9},{9,8},{10,11... | collective-permute-start | bytes 1572872 | tf_op jit(solution)/shard_map/ppermute | solution.py:102
  311.1 23.7 %collective-permute-start.93 = (bf16[1024,512]{1,0:T(8,128)(2,1)S(1)}, bf16[1024,512]{1,0:T(8,128)(2,1)}, u32[]{:S(2)}, u32[]{:S(2)}) collective-permute-start(bf16[1024,512]{1,0:T(8,128)(2,1)S(1)} %constant_dynamic-update-slice_fusion.64.refs_0_), channel_id=1, source_target_pairs={{0,1},{1,0},{2,3},{3,2},{4,5},{5,4},{6,7},{7,6},{8,9},{9,8},{10,11... | collective-permute-start | bytes 3145736 | tf_op jit(solution)/shard_map/ppermute | solution.py:102
  311.1 28.4 %collective-permute-start.81 = (bf16[1024,512]{1,0:T(8,128)(2,1)}, bf16[1024,512]{1,0:T(8,128)(2,1)}, u32[]{:S(2)}, u32[]{:S(2)}) collective-permute-start(bf16[1024,512]{1,0:T(8,128)(2,1)} %constant_dynamic-update-slice_fusion.53.refs_0_), channel_id=1, source_target_pairs={{0,1},{1,0},{2,3},{3,2},{4,5},{5,4},{6,7},{7,6},{8,9},{9,8},{10,11... | collective-permute-start | bytes 3145736 | tf_op jit(solution)/shard_map/ppermute | solution.py:102
  317.6 12.9 %collective-permute-start.27 = (bf16[512,512]{1,0:T(8,128)(2,1)S(1)}, bf16[512,512]{1,0:T(8,128)(2,1)}, u32[]{:S(2)}, u32[]{:S(2)}) collective-permute-start(bf16[512,512]{1,0:T(8,128)(2,1)S(1)} %constant_dynamic-update-slice_fusion.5.refs_0_), channel_id=1, source_target_pairs={{0,1},{1,0},{2,3},{3,2},{4,5},{5,4},{6,7},{7,6},{8,9},{9,8},{10,11... | collective-permute-start | bytes 1572872 | tf_op jit(solution)/shard_map/ppermute | solution.py:102
  (93 other events, 708.5 us)
